TPU v7x, 128 devices: a whole 4x4x4 slice. The times are simulated.
128 devices in a mesh: dp: 2 (over core), gy: 8 (over x, z_hi), gx: 8 (over y, z_lo).
Axes of the slice: x: 4, y: 4, z: 4 (z_hi: 2, z_lo: 2; z = z_hi * 2 + z_lo), core: 2. Of those that a mesh axis runs over, the one named last changes fastest.
Arguments:
- fine_input: bfloat16 [2, 8, 128, 9216], P('dp', None, 'gy', 'gx'), may hold values from -6 to 6
- fine_weight: bfloat16 [3, 3, 72, 72], replicated, may hold values from -0.25 to 0.25
- entry_weight: bfloat16 [3, 3, 3, 72, 96], replicated, may hold values from -0.125 to 0.125
- middle_weight: bfloat16 [3, 3, 3, 96, 96], replicated, may hold values from -0.125 to 0.125
- lift_weight: bfloat16 [96, 72], replicated, may hold values from -0.625 to 0.625
- upstream: bfloat16 [2, 8, 128, 9216], P('dp', None, 'gy', 'gx'), may hold values from -6 to 6
Outputs:
- mixed: bfloat16 [2, 8, 128, 9216], P('dp', None, 'gy', 'gx')
- input_grad: bfloat16 [2, 8, 128, 9216], P('dp', None, 'gy', 'gx')
- fine_weight_grad: float32 [3, 3, 72, 72], replicated
- entry_weight_grad: float32 [3, 3, 3, 72, 96], replicated
- middle_weight_grad: float32 [3, 3, 3, 96, 96], replicated
- lift_weight_grad: float32 [96, 72], replicated
All inputs are finite; a program needn't handle non-finite values.
Results may differ from a plain program's by a relative error of at most 0.018.
Values may be sent and summed in bfloat16 or wider, within the bound.
A program may use at most 128 MiB of HBM per device.

v0:
```python
import jax
import jax.numpy as jnp
from jax import lax
from jax.sharding import PartitionSpec as P


def padded_2(block, sides, width):
    for axis, dim in sides:
        count = lax.axis_size(axis)
        forward = [(i, i + 1) for i in range(count - 1)]
        backward = [(target, source) for source, target in forward]
        low = lax.ppermute(
            lax.slice_in_dim(block, block.shape[dim] - width, None, axis=dim), axis, forward
        )
        high = lax.ppermute(lax.slice_in_dim(block, 0, width, axis=dim), axis, backward)
        block = jnp.concatenate([low, block, high], axis=dim)
    return block


def activate(values):
    return jnp.where(values > 0, values, jnp.expm1(jnp.minimum(values, 0.0)))


def activation_slope(stored):
    widened = stored.astype(jnp.float32)
    return jnp.where(widened > 0, 1.0, 1.0 + widened)


def conv_taps(padded, weight, cell_shape):
    count, depth, row_count, col_count = cell_shape
    kernel_depth = weight.shape[0]
    channels = weight.shape[3]
    outputs = weight.shape[4]
    summed = jnp.zeros((count * depth * row_count * col_count, outputs), jnp.float32)
    for z_tap in range(kernel_depth):
        for y_tap in range(3):
            stacked = jnp.concatenate(
                [
                    padded[
                        :,
                        z_tap : z_tap + depth,
                        y_tap : y_tap + row_count,
                        x_tap : x_tap + col_count,
                        :,
                    ]
                    for x_tap in range(3)
                ],
                axis=-1,
            )
            summed = summed + jnp.dot(
                stacked.reshape(-1, 3 * channels),
                weight[z_tap, y_tap].reshape(3 * channels, outputs),
                preferred_element_type=jnp.float32,
            )
    return summed.reshape(count, depth, row_count, col_count, outputs)


def weight_grad(padded, gradient, kernel_depth):
    count, depth, row_count, col_count, outputs = gradient.shape
    channels = padded.shape[-1]
    flattened = gradient.reshape(-1, outputs)
    pieces = []
    for z_tap in range(kernel_depth):
        for y_tap in range(3):
            stacked = jnp.concatenate(
                [
                    padded[
                        :,
                        z_tap : z_tap + depth,
                        y_tap : y_tap + row_count,
                        x_tap : x_tap + col_count,
                        :,
                    ]
                    for x_tap in range(3)
                ],
                axis=-1,
            )
            product = lax.dot_general(
                stacked.reshape(-1, 3 * channels),
                flattened,
                (((0,), (0,)), ((), ())),
                preferred_element_type=jnp.float32,
            )
            pieces.append(product.reshape(3, channels, outputs))
    return jnp.stack(pieces).reshape(kernel_depth, 3, 3, channels, outputs)


def flipped(weight):
    return jnp.swapaxes(jnp.flip(weight, axis=(0, 1, 2)), 3, 4)


def pool_sum(values):
    count, depth, row_count, col_count, channels = values.shape
    grouped = values.astype(jnp.float32).reshape(
        count, depth, row_count // 2, 2, col_count // 2, 2, channels
    )
    return grouped.sum(axis=(3, 5))


def upsample(values):
    return jnp.repeat(jnp.repeat(values, 2, axis=2), 2, axis=3)


def depth_pad(values):
    return jnp.pad(values, ((0, 0), (1, 1), (0, 0), (0, 0), (0, 0)))


def body(fine_input, fine_weight, entry_weight, middle_weight, lift_weight, upstream):
    count, depth, row_count, merged = fine_input.shape
    channels = fine_weight.shape[2]
    wide = lift_weight.shape[0]
    col_count = merged // channels
    fine_shape = (count, depth, row_count, col_count)
    low_shape = (count, depth, row_count // 2, col_count // 2)
    features = fine_input.reshape(count, depth, row_count, col_count, channels)
    upstream_cells = upstream.reshape(count, depth, row_count, col_count, channels)
    kernel_fine = fine_weight[None]

    def fine_pad(values):
        return padded_2(values, (("gy", 2), ("gx", 3)), 1)

    padded_in = fine_pad(features)
    fine_act = activate(conv_taps(padded_in, kernel_fine, fine_shape)).astype(jnp.bfloat16)
    pooled = (0.25 * pool_sum(fine_act)).astype(jnp.bfloat16)

    def coarse_pad(values):
        return depth_pad(padded_2(values, (("gy", 2), ("gx", 3)), 1))

    pooled_pad = coarse_pad(pooled)
    coarse_one = activate(conv_taps(pooled_pad, entry_weight, low_shape)).astype(jnp.bfloat16)
    one_pad = coarse_pad(coarse_one)
    coarse_two = activate(conv_taps(one_pad, middle_weight, low_shape)).astype(jnp.bfloat16)
    low_cells = coarse_two.reshape(-1, wide)
    lifted = (
        jnp.dot(low_cells, lift_weight, preferred_element_type=jnp.float32)
        .astype(jnp.bfloat16)
        .reshape(low_shape + (channels,))
    )
    mixed = (fine_act.astype(jnp.float32) + upsample(lifted).astype(jnp.float32)).astype(
        jnp.bfloat16
    )
    upstream_low = pool_sum(upstream_cells).astype(jnp.bfloat16)
    low_grad = upstream_low.reshape(-1, channels)
    lift_grad = lax.dot_general(
        low_cells, low_grad, (((0,), (0,)), ((), ())), preferred_element_type=jnp.float32
    )
    back_lift = lax.dot_general(
        low_grad, lift_weight, (((1,), (1,)), ((), ())), preferred_element_type=jnp.float32
    )
    grad_two = (back_lift.reshape(low_shape + (wide,)) * activation_slope(coarse_two)).astype(
        jnp.bfloat16
    )
    middle_grad = weight_grad(one_pad, grad_two, 3)
    grad_one = (
        conv_taps(coarse_pad(grad_two), flipped(middle_weight), low_shape)
        * activation_slope(coarse_one)
    ).astype(jnp.bfloat16)
    grad_one_pad = coarse_pad(grad_one)
    entry_grad = weight_grad(pooled_pad, grad_one, 3)
    grad_pool = conv_taps(grad_one_pad, flipped(entry_weight), low_shape).astype(jnp.bfloat16)
    grad_fine_pre = (
        (upstream_cells.astype(jnp.float32) + 0.25 * upsample(grad_pool).astype(jnp.float32))
        * activation_slope(fine_act)
    ).astype(jnp.bfloat16)
    fine_grad = weight_grad(padded_in, grad_fine_pre, 1)[0]
    grad_input = conv_taps(fine_pad(grad_fine_pre), flipped(kernel_fine), fine_shape).astype(
        jnp.bfloat16
    )
    fine_grad, entry_grad, middle_grad, lift_grad = lax.psum(
        (fine_grad, entry_grad, middle_grad, lift_grad), ("dp", "gy", "gx")
    )
    return (
        mixed.reshape(fine_input.shape),
        grad_input.reshape(fine_input.shape),
        fine_grad,
        entry_grad,
        middle_grad,
        lift_grad,
    )


def solution(mesh):
    return jax.shard_map(
        body,
        mesh=mesh,
        in_specs=(P("dp", None, "gy", "gx"), P(), P(), P(), P(), P("dp", None, "gy", "gx")),
        out_specs=(P("dp", None, "gy", "gx"), P("dp", None, "gy", "gx"), P(), P(), P(), P()),
        check_vma=False,
    )
```

profile of v0, /device:TPU:1, one launch (start us, length us, event | category | flops | bytes accessed | tf_op | source)
XLA Modules:
  0.0 484.4 jit_solution(6377397240401198821)
XLA Ops:
  7.2 2.0 reshape.768
  9.2 6.3 %collective-permute-start = (bf16[1,8,1,16,72]{4,3,2,1,0:T(8,128)(2,1)S(1)}, bf16[1,8,1,16,72]{4,3,2,1,0:T(8,128)(2,1)S(1)}, u32[]{:S(2)}, u32[]{:S(2)}) collective-permute-start(bf16[1,8,1,16,72]{4,3,2,1,0:T(8,128)(2,1)S(1)} %get-tuple-element.52), channel_id=1, source_target_pairs={{0,8},{8,16},{16,24},{24,32},{32,40},{40,48},{48,56},{1,9},{9,17},... | collective-permute-start | bytes 55304 | tf_op jit(solution)/shard_map/ppermute | solution.py:12
  22.0 2.6 collective-permute-start.2
  27.0 3.1 collective-permute-done.3
  30.9 3.1 fusion.33
  37.9 2.4 convert_reduce_fusion
  41.7 5.5 %collective-permute-start.4 = (bf16[1,8,1,8,72]{4,3,2,1,0:T(8,128)(2,1)}, bf16[1,8,1,8,72]{4,3,2,1,0:T(8,128)(2,1)S(1)}, u32[]{:S(2)}, u32[]{:S(2)}) collective-permute-start(bf16[1,8,1,8,72]{4,3,2,1,0:T(8,128)(2,1)} %get-tuple-element.203), channel_id=1, source_target_pairs={{0,8},{8,16},{16,24},{24,32},{32,40},{40,48},{48,56},{1,9},{9,17},... | collective-permute-start | bytes 27656 | tf_op jit(solution)/shard_map/ppermute | solution.py:12
  49.3 2.7 reshape.790
  52.0 2.8 reshape.837
  54.8 2.8 reshape.836
  71.1 2.4 copy.125
  75.6 2.7 reduce_sum.22
  78.4 3.3 collective-permute-start.6
  84.0 2.5 collective-permute-done.7
  96.7 6.1 %collective-permute-start.8 = (bf16[1,8,1,8,96]{4,3,2,1,0:T(8,128)(2,1)}, bf16[1,8,1,8,96]{4,3,2,1,0:T(8,128)(2,1)S(1)}, u32[]{:S(2)}, u32[]{:S(2)}) collective-permute-start(bf16[1,8,1,8,96]{4,3,2,1,0:T(8,128)(2,1)} %get-tuple-element.199), channel_id=1, source_target_pairs={{0,8},{8,16},{16,24},{24,32},{32,40},{40,48},{48,56},{1,9},{9,17},... | collective-permute-start | bytes 36872 | tf_op jit(solution)/shard_map/ppermute | solution.py:12
  104.1 2.9 fusion.103
  109.6 2.2 copy.133
  114.6 3.4 collective-permute-start.10
  151.7 6.1 %collective-permute-start.12 = (bf16[1,8,1,8,96]{4,3,2,1,0:T(8,128)(2,1)}, bf16[1,8,1,8,96]{4,3,2,1,0:T(8,128)(2,1)S(1)}, u32[]{:S(2)}, u32[]{:S(2)}) collective-permute-start(bf16[1,8,1,8,96]{4,3,2,1,0:T(8,128)(2,1)} %get-tuple-element.195), channel_id=1, source_target_pairs={{0,8},{8,16},{16,24},{24,32},{32,40},{40,48},{48,56},{1,9},{9,17},... | collective-permute-start | bytes 36872 | tf_op jit(solution)/shard_map/ppermute | solution.py:12
  173.4 3.4 collective-permute-start.14
  178.4 76.7 %psum.31 = f32[96,72]{0,1:T(8,128)} all-reduce(f32[96,72]{0,1:T(8,128)S(1)} %convolution_bitcast_fusion.21), channel_id=1, replica_groups=mesh['dp'=2,'gy'=8,'gx'=8] {'dp','gy','gx'}, use_global_device_ids=true, to_apply=%region_5.6 | all-reduce | flops 6912 | bytes 55296 | tf_op jit(solution)/shard_map/psum | solution.py:169
  262.0 3.2 collective-permute-start.16
  268.3 2.9 collective-permute-done.17
  271.2 2.8 collective-permute-start.18
  276.6 2.3 collective-permute-done.19
  298.1 4.1 collective-permute-start.20
  303.9 4.4 collective-permute-done.21
  308.5 3.6 collective-permute-start.22
  314.3 3.0 collective-permute-done.23
  323.9 2.1 fusion.30
  329.4 142.8 %all-reduce.7.cloned.1.call-done = (f32[3,3,72,72]{3,2,1,0:T(8,128)}, f32[3,3,3,72,96]{4,3,2,1,0:T(8,128)}, f32[3,3,3,96,96]{4,3,2,1,0:T(8,128)}) async-done(((f32[3,3,72,72]{3,2,1,0:T(8,128)}, f32[3,3,3,72,96]{4,3,2,1,0:T(8,128)}, f32[3,3,3,96,96]{4,3,2,1,0:T(8,128)}), (f32[3,3,72,72]{3,2,1,0:T(8,128)}, f32[3,3,3,72,96]{4,3,2,1,0:T(8,128)}, f32[3,3,3,96,96]{4,3,2,1,0:T(8,128)})) %all-reduce.7.cloned.1.call-update) | async-done | bytes 1928464 | tf_op jit(solution)/shard_map/psum | solution.py:169
  474.0 2.2 copy.207
  (498 shorter events, 149.4 us)
Async XLA Ops:
  7.2 143.5 %copy-start = (bf16[96,72]{0,1:T(8,128)(2,1)S(1)}, bf16[96,72]{0,1:T(8,128)(2,1)}, u32[]{:S(2)}) copy-start(bf16[96,72]{0,1:T(8,128)(2,1)} %param.10) | copy-start | bytes 41476
  7.2 9.8 %copy-start.14 = (bf16[3,3,3,96,96]{4,3,2,1,0:T(8,128)(2,1)S(1)}, bf16[3,3,3,96,96]{4,3,2,1,0:T(8,128)(2,1)}, u32[]{:S(2)}) copy-start(bf16[3,3,3,96,96]{4,3,2,1,0:T(8,128)(2,1)} %param.9) | copy-start | bytes 1492996
  7.2 465.0 %all-reduce.7.cloned.1.call-start = ((), (), s32[]{:S(2)}) async-start(), calls=%async_computation | async-start | bytes 5308416 | tf_op jit(solution)/shard_map/psum | solution.py:169
  9.2 12.2 %collective-permute-start = (bf16[1,8,1,16,72]{4,3,2,1,0:T(8,128)(2,1)S(1)}, bf16[1,8,1,16,72]{4,3,2,1,0:T(8,128)(2,1)S(1)}, u32[]{:S(2)}, u32[]{:S(2)}) collective-permute-start(bf16[1,8,1,16,72]{4,3,2,1,0:T(8,128)(2,1)S(1)} %get-tuple-element.52), channel_id=1, source_target_pairs={{0,8},{8,16},{16,24},{24,32},{32,40},{40,48},{48,56},{1,9},{9,17},... | collective-permute-start | bytes 55304 | tf_op jit(solution)/shard_map/ppermute | solution.py:12
  15.6 6.3 %collective-permute-start.1 = (bf16[1,8,1,16,72]{4,3,2,1,0:T(8,128)(2,1)S(1)}, bf16[1,8,1,16,72]{4,3,2,1,0:T(8,128)(2,1)S(1)}, u32[]{:S(2)}, u32[]{:S(2)}) collective-permute-start(bf16[1,8,1,16,72]{4,3,2,1,0:T(8,128)(2,1)S(1)} %get-tuple-element.51), channel_id=1, source_target_pairs={{8,0},{16,8},{24,16},{32,24},{40,32},{48,40},{56,48},{9,1},{17,9},... | collective-permute-start | bytes 55304 | tf_op jit(solution)/shard_map/ppermute | solution.py:15
  21.4 9.4 %copy-start.117 = (bf16[1,8,1,16,72]{4,3,2,1,0:T(8,128)(2,1)}, bf16[1,8,1,16,72]{4,3,2,1,0:T(8,128)(2,1)S(1)}, u32[]{:S(2)}) copy-start(bf16[1,8,1,16,72]{4,3,2,1,0:T(8,128)(2,1)S(1)} %collective-permute-done) | copy-start | bytes 55300
  21.9 9.0 %copy-start.118 = (bf16[1,8,1,16,72]{4,3,2,1,0:T(8,128)(2,1)}, bf16[1,8,1,16,72]{4,3,2,1,0:T(8,128)(2,1)S(1)}, u32[]{:S(2)}) copy-start(bf16[1,8,1,16,72]{4,3,2,1,0:T(8,128)(2,1)S(1)} %collective-permute-done.1) | copy-start | bytes 55300
  22.0 4.9 %collective-permute-start.2 = (bf16[1,8,18,1,72]{4,3,2,1,0:T(2,128)(2,1)S(1)}, bf16[1,8,18,1,72]{4,3,2,1,0:T(2,128)(2,1)S(1)}, u32[]{:S(2)}, u32[]{:S(2)}) collective-permute-start(bf16[1,8,18,1,72]{4,3,2,1,0:T(2,128)(2,1)S(1)} %get-tuple-element.43), channel_id=1, source_target_pairs={{0,1},{1,2},{2,3},{3,4},{4,5},{5,6},{6,7},{8,9},{9,10},{10,11},{11... | collective-permute-start | bytes 62216 | tf_op jit(solution)/shard_map/ppermute | solution.py:12
  24.7 5.4 %collective-permute-start.3 = (bf16[1,8,18,1,72]{4,3,2,1,0:T(2,128)(2,1)S(1)}, bf16[1,8,18,1,72]{4,3,2,1,0:T(2,128)(2,1)S(1)}, u32[]{:S(2)}, u32[]{:S(2)}) collective-permute-start(bf16[1,8,18,1,72]{4,3,2,1,0:T(2,128)(2,1)S(1)} %get-tuple-element.44), channel_id=1, source_target_pairs={{1,0},{2,1},{3,2},{4,3},{5,4},{6,5},{7,6},{9,8},{10,9},{11,10},{12... | collective-permute-start | bytes 62216 | tf_op jit(solution)/shard_map/ppermute | solution.py:15
  41.7 36.6 %collective-permute-start.4 = (bf16[1,8,1,8,72]{4,3,2,1,0:T(8,128)(2,1)}, bf16[1,8,1,8,72]{4,3,2,1,0:T(8,128)(2,1)S(1)}, u32[]{:S(2)}, u32[]{:S(2)}) collective-permute-start(bf16[1,8,1,8,72]{4,3,2,1,0:T(8,128)(2,1)} %get-tuple-element.203), channel_id=1, source_target_pairs={{0,8},{8,16},{16,24},{24,32},{32,40},{40,48},{48,56},{1,9},{9,17},... | collective-permute-start | bytes 27656 | tf_op jit(solution)/shard_map/ppermute | solution.py:12
  47.2 31.1 %collective-permute-start.5 = (bf16[1,8,1,8,72]{4,3,2,1,0:T(8,128)(2,1)}, bf16[1,8,1,8,72]{4,3,2,1,0:T(8,128)(2,1)S(1)}, u32[]{:S(2)}, u32[]{:S(2)}) collective-permute-start(bf16[1,8,1,8,72]{4,3,2,1,0:T(8,128)(2,1)} %get-tuple-element.204), channel_id=1, source_target_pairs={{8,0},{16,8},{24,16},{32,24},{40,32},{48,40},{56,48},{9,1},{17,9},... | collective-permute-start | bytes 27656 | tf_op jit(solution)/shard_map/ppermute | solution.py:15
  54.8 10.7 %copy-start.109 = (bf16[1,1,3,96,72]{3,4,2,1,0:T(8,128)(2,1)S(1)}, bf16[1,1,3,96,72]{3,4,2,1,0:T(8,128)(2,1)}, u32[]{:S(2)}) copy-start(bf16[1,1,3,96,72]{3,4,2,1,0:T(8,128)(2,1)} %get-tuple-element.56) | copy-start | bytes 124420
  78.4 5.6 %collective-permute-start.6 = (bf16[1,8,10,1,72]{4,3,2,1,0:T(2,128)(2,1)S(1)}, bf16[1,8,10,1,72]{4,3,2,1,0:T(2,128)(2,1)S(1)}, u32[]{:S(2)}, u32[]{:S(2)}) collective-permute-start(bf16[1,8,10,1,72]{4,3,2,1,0:T(2,128)(2,1)S(1)} %get-tuple-element.187), channel_id=1, source_target_pairs={{0,1},{1,2},{2,3},{3,4},{4,5},{5,6},{6,7},{8,9},{9,10},{10,11},{11... | collective-permute-start | bytes 34568 | tf_op jit(solution)/shard_map/ppermute | solution.py:12
  81.7 4.7 collective-permute-start.7
  96.7 16.5 %collective-permute-start.8 = (bf16[1,8,1,8,96]{4,3,2,1,0:T(8,128)(2,1)}, bf16[1,8,1,8,96]{4,3,2,1,0:T(8,128)(2,1)S(1)}, u32[]{:S(2)}, u32[]{:S(2)}) collective-permute-start(bf16[1,8,1,8,96]{4,3,2,1,0:T(8,128)(2,1)} %get-tuple-element.199), channel_id=1, source_target_pairs={{0,8},{8,16},{16,24},{24,32},{32,40},{40,48},{48,56},{1,9},{9,17},... | collective-permute-start | bytes 36872 | tf_op jit(solution)/shard_map/ppermute | solution.py:12
  102.8 10.4 %collective-permute-start.9 = (bf16[1,8,1,8,96]{4,3,2,1,0:T(8,128)(2,1)}, bf16[1,8,1,8,96]{4,3,2,1,0:T(8,128)(2,1)}, u32[]{:S(2)}, u32[]{:S(2)}) collective-permute-start(bf16[1,8,1,8,96]{4,3,2,1,0:T(8,128)(2,1)} %get-tuple-element.200), channel_id=1, source_target_pairs={{8,0},{16,8},{24,16},{32,24},{40,32},{48,40},{56,48},{9,1},{17,9},... | collective-permute-start | bytes 36872 | tf_op jit(solution)/shard_map/ppermute | solution.py:15
  111.8 9.5 %copy-start.23 = (bf16[1,8,8,8,216]{4,3,2,1,0:T(8,128)(2,1)S(1)}, bf16[1,8,8,8,216]{4,3,2,1,0:T(8,128)(2,1)}, u32[]{:S(2)}) copy-start(bf16[1,8,8,8,216]{4,3,2,1,0:T(8,128)(2,1)} %copy-done.22) | copy-start | bytes 663556
  113.1 9.8 %copy-start.31 = (bf16[1,8,8,8,216]{4,3,2,1,0:T(8,128)(2,1)S(1)}, bf16[1,8,8,8,216]{4,3,2,1,0:T(8,128)(2,1)}, u32[]{:S(2)}) copy-start(bf16[1,8,8,8,216]{4,3,2,1,0:T(8,128)(2,1)} %copy-done.30) | copy-start | bytes 663556
  114.6 13.2 %collective-permute-start.10 = (bf16[1,8,10,1,96]{4,3,2,1,0:T(2,128)(2,1)}, bf16[1,8,10,1,96]{4,3,2,1,0:T(2,128)(2,1)}, u32[]{:S(2)}, u32[]{:S(2)}) collective-permute-start(bf16[1,8,10,1,96]{4,3,2,1,0:T(2,128)(2,1)} %get-tuple-element.183), channel_id=1, source_target_pairs={{0,1},{1,2},{2,3},{3,4},{4,5},{5,6},{6,7},{8,9},{9,10},{10,11},{11... | collective-permute-start | bytes 46088 | tf_op jit(solution)/shard_map/ppermute | solution.py:12
  118.0 9.8 %collective-permute-start.11 = (bf16[1,8,10,1,96]{4,3,2,1,0:T(2,128)(2,1)}, bf16[1,8,10,1,96]{4,3,2,1,0:T(2,128)(2,1)}, u32[]{:S(2)}, u32[]{:S(2)}) collective-permute-start(bf16[1,8,10,1,96]{4,3,2,1,0:T(2,128)(2,1)} %get-tuple-element.184), channel_id=1, source_target_pairs={{1,0},{2,1},{3,2},{4,3},{5,4},{6,5},{7,6},{9,8},{10,9},{11,10},{12... | collective-permute-start | bytes 46088 | tf_op jit(solution)/shard_map/ppermute | solution.py:15
  151.7 21.6 %collective-permute-start.12 = (bf16[1,8,1,8,96]{4,3,2,1,0:T(8,128)(2,1)}, bf16[1,8,1,8,96]{4,3,2,1,0:T(8,128)(2,1)S(1)}, u32[]{:S(2)}, u32[]{:S(2)}) collective-permute-start(bf16[1,8,1,8,96]{4,3,2,1,0:T(8,128)(2,1)} %get-tuple-element.195), channel_id=1, source_target_pairs={{0,8},{8,16},{16,24},{24,32},{32,40},{40,48},{48,56},{1,9},{9,17},... | collective-permute-start | bytes 36872 | tf_op jit(solution)/shard_map/ppermute | solution.py:12
  157.8 15.5 %collective-permute-start.13 = (bf16[1,8,1,8,96]{4,3,2,1,0:T(8,128)(2,1)}, bf16[1,8,1,8,96]{4,3,2,1,0:T(8,128)(2,1)S(1)}, u32[]{:S(2)}, u32[]{:S(2)}) collective-permute-start(bf16[1,8,1,8,96]{4,3,2,1,0:T(8,128)(2,1)} %get-tuple-element.196), channel_id=1, source_target_pairs={{8,0},{16,8},{24,16},{32,24},{40,32},{48,40},{56,48},{9,1},{17,9},... | collective-permute-start | bytes 36872 | tf_op jit(solution)/shard_map/ppermute | solution.py:15
  173.4 81.7 %collective-permute-start.14 = (bf16[1,8,10,1,96]{4,3,2,1,0:T(2,128)(2,1)S(1)}, bf16[1,8,10,1,96]{4,3,2,1,0:T(2,128)(2,1)S(1)}, u32[]{:S(2)}, u32[]{:S(2)}) collective-permute-start(bf16[1,8,10,1,96]{4,3,2,1,0:T(2,128)(2,1)S(1)} %get-tuple-element.179), channel_id=1, source_target_pairs={{0,1},{1,2},{2,3},{3,4},{4,5},{5,6},{6,7},{8,9},{9,10},{10,11},{11... | collective-permute-start | bytes 46088 | tf_op jit(solution)/shard_map/ppermute | solution.py:12
  176.8 78.3 %collective-permute-start.15 = (bf16[1,8,10,1,96]{4,3,2,1,0:T(2,128)(2,1)S(1)}, bf16[1,8,10,1,96]{4,3,2,1,0:T(2,128)(2,1)S(1)}, u32[]{:S(2)}, u32[]{:S(2)}) collective-permute-start(bf16[1,8,10,1,96]{4,3,2,1,0:T(2,128)(2,1)S(1)} %get-tuple-element.180), channel_id=1, source_target_pairs={{1,0},{2,1},{3,2},{4,3},{5,4},{6,5},{7,6},{9,8},{10,9},{11,10},{12... | collective-permute-start | bytes 46088 | tf_op jit(solution)/shard_map/ppermute | solution.py:15
  262.0 6.3 %collective-permute-start.16 = (bf16[1,8,1,8,96]{4,3,2,1,0:T(8,128)(2,1)S(1)}, bf16[1,8,1,8,96]{4,3,2,1,0:T(8,128)(2,1)S(1)}, u32[]{:S(2)}, u32[]{:S(2)}) collective-permute-start(bf16[1,8,1,8,96]{4,3,2,1,0:T(8,128)(2,1)S(1)} %get-tuple-element.191), channel_id=1, source_target_pairs={{0,8},{8,16},{16,24},{24,32},{32,40},{40,48},{48,56},{1,9},{9,17},... | collective-permute-start | bytes 36872 | tf_op jit(solution)/shard_map/ppermute | solution.py:12
  265.2 6.0 %collective-permute-start.17 = (bf16[1,8,1,8,96]{4,3,2,1,0:T(8,128)(2,1)S(1)}, bf16[1,8,1,8,96]{4,3,2,1,0:T(8,128)(2,1)S(1)}, u32[]{:S(2)}, u32[]{:S(2)}) collective-permute-start(bf16[1,8,1,8,96]{4,3,2,1,0:T(8,128)(2,1)S(1)} %get-tuple-element.192), channel_id=1, source_target_pairs={{8,0},{16,8},{24,16},{32,24},{40,32},{48,40},{56,48},{9,1},{17,9},... | collective-permute-start | bytes 36872 | tf_op jit(solution)/shard_map/ppermute | solution.py:15
  271.2 4.5 collective-permute-start.18
  274.0 5.0 %collective-permute-start.19 = (bf16[1,8,10,1,96]{4,3,2,1,0:T(2,128)(2,1)S(1)}, bf16[1,8,10,1,96]{4,3,2,1,0:T(2,128)(2,1)S(1)}, u32[]{:S(2)}, u32[]{:S(2)}) collective-permute-start(bf16[1,8,10,1,96]{4,3,2,1,0:T(2,128)(2,1)S(1)} %get-tuple-element.176), channel_id=1, source_target_pairs={{1,0},{2,1},{3,2},{4,3},{5,4},{6,5},{7,6},{9,8},{10,9},{11,10},{12... | collective-permute-start | bytes 46088 | tf_op jit(solution)/shard_map/ppermute | solution.py:15
  298.1 5.9 %collective-permute-start.20 = (bf16[1,8,1,16,72]{4,3,2,1,0:T(8,128)(2,1)S(1)}, bf16[1,8,1,16,72]{4,3,2,1,0:T(8,128)(2,1)S(1)}, u32[]{:S(2)}, u32[]{:S(2)}) collective-permute-start(bf16[1,8,1,16,72]{4,3,2,1,0:T(8,128)(2,1)S(1)} %get-tuple-element.48), channel_id=1, source_target_pairs={{0,8},{8,16},{16,24},{24,32},{32,40},{40,48},{48,56},{1,9},{9,17},... | collective-permute-start | bytes 55304 | tf_op jit(solution)/shard_map/ppermute | solution.py:12
  302.2 6.2 %collective-permute-start.21 = (bf16[1,8,1,16,72]{4,3,2,1,0:T(8,128)(2,1)S(1)}, bf16[1,8,1,16,72]{4,3,2,1,0:T(8,128)(2,1)S(1)}, u32[]{:S(2)}, u32[]{:S(2)}) collective-permute-start(bf16[1,8,1,16,72]{4,3,2,1,0:T(8,128)(2,1)S(1)} %get-tuple-element.47), channel_id=1, source_target_pairs={{8,0},{16,8},{24,16},{32,24},{40,32},{48,40},{56,48},{9,1},{17,9},... | collective-permute-start | bytes 55304 | tf_op jit(solution)/shard_map/ppermute | solution.py:15
  308.5 5.7 %collective-permute-start.22 = (bf16[1,8,18,1,72]{4,3,2,1,0:T(2,128)(2,1)S(1)}, bf16[1,8,18,1,72]{4,3,2,1,0:T(2,128)(2,1)S(1)}, u32[]{:S(2)}, u32[]{:S(2)}) collective-permute-start(bf16[1,8,18,1,72]{4,3,2,1,0:T(2,128)(2,1)S(1)} %get-tuple-element.39), channel_id=1, source_target_pairs={{0,1},{1,2},{2,3},{3,4},{4,5},{5,6},{6,7},{8,9},{9,10},{10,11},{11... | collective-permute-start | bytes 62216 | tf_op jit(solution)/shard_map/ppermute | solution.py:12
  312.2 5.1 %collective-permute-start.23 = (bf16[1,8,18,1,72]{4,3,2,1,0:T(2,128)(2,1)S(1)}, bf16[1,8,18,1,72]{4,3,2,1,0:T(2,128)(2,1)S(1)}, u32[]{:S(2)}, u32[]{:S(2)}) collective-permute-start(bf16[1,8,18,1,72]{4,3,2,1,0:T(2,128)(2,1)S(1)} %get-tuple-element.40), channel_id=1, source_target_pairs={{1,0},{2,1},{3,2},{4,3},{5,4},{6,5},{7,6},{9,8},{10,9},{11,10},{12... | collective-permute-start | bytes 62216 | tf_op jit(solution)/shard_map/ppermute | solution.py:15
  (118 other events, 312.3 us)
Sparse Core Ops, SparseCore 0:
  314.4 157.8 all-reduce.6
where the time goes:
time: 494 us; the launch traced here: 484 us
  waiting for transfers between devices  161 us (33%)
  local copies, waits for them, and re-layouts  96.1 us (19%)
  blocking collectives  76.7 us (16%)
  starting transfers between devices  66.7 us (14%)
  other arithmetic  36.1 us (7%)
  matrix products  31 us (6%)
  between operations  16.3 us (3%)
    psum x1, waiting for transfers between devices, body(): lax.psum((fine_grad, entry_grad, middle_grad, lift_grad), ('dp', 'gy', 'g...  143 us
    psum x1, blocking collectives, body(): lax.psum((fine_grad, entry_grad, middle_grad, lift_grad), ('dp', 'gy', 'g...  76.7 us
    ppermute x12, starting transfers between devices, padded_2(): lax.ppermute(lax.slice_in_dim(block, block.shape[dim] - width, None, axis...  50.5 us
    dot_general x20, local copies, waits for them, and re-layouts, weight_grad(): lax.dot_general(stacked.reshape(-1, 3 * channels), flattened, (((0,), (0,...  18.9 us
    ppermute x12, waiting for transfers between devices, padded_2(): lax.ppermute(lax.slice_in_dim(block, 0, width, axis=dim), axis, backward)  18.6 us
    dot_general x42, matrix products, conv_taps(): jnp.dot(stacked.reshape(-1, 3 * channels), weight[z_tap, y_tap].reshape(3...  16.2 us
    ppermute x12, starting transfers between devices, padded_2(): lax.ppermute(lax.slice_in_dim(block, 0, width, axis=dim), axis, backward)  16.2 us
    concatenate x28, other arithmetic, conv_taps(): jnp.concatenate([padded[:, z_tap:z_tap + depth, y_tap:y_tap + row_count,...  14.3 us
  transfers between devices with their start and end apart: 25, of which 8 were waited for; matrix products, arithmetic and copies ran while one was open for 17% of the time, Pallas kernels for 0%

commit v1 on v0

v1 whole, which is shorter than its diff:
```python
import functools

import jax
import jax.numpy as jnp
from jax import lax
from jax.experimental import pallas as pl
from jax.experimental.pallas import tpu as pltpu
from jax.sharding import PartitionSpec as P

MESH = pl.DeviceIdType.MESH
BF = jnp.bfloat16
F32 = jnp.float32

Z = 8
N2 = 16
N3 = 8
C2 = 72
C3 = 96
L = 128
GY = 8
GX = 8
MERGED = N2 * C2
TILES = MERGED // L
DIRS = [(dy, dx) for dy in (-1, 0, 1) for dx in (-1, 0, 1) if (dy, dx) != (0, 0)]

EX_IN, EX_POOL, EX_ONE, EX_G2, EX_G1, EX_FINE = range(6)

ROWS_M = 2048
ROWS_E = 1536
ROWS_F = 512


def lanes(shape):
    return lax.broadcasted_iota(jnp.int32, shape, len(shape) - 1)


def elu(v):
    return jnp.where(v > 0, v, jnp.exp(jnp.minimum(v, 0.0)) - 1.0)


def slope(s):
    return jnp.where(s > 0, 1.0, 1.0 + s)


def rounded(v):
    return v.astype(BF).astype(F32)


def shift_z(v, step):
    moved = pltpu.roll(v, step % Z, 1)
    row = lax.broadcasted_iota(jnp.int32, v.shape, 1)
    return jnp.where(row == (0 if step == 1 else Z - 1), 0.0, moved)


def nt(a, b):
    return lax.dot_general(a, b, (((1,), (1,)), ((), ())), preferred_element_type=F32)


def nn(a, b):
    return jnp.dot(a, b, preferred_element_type=F32)


class Ring:
    def __init__(self):
        self.dp = lax.axis_index("dp")
        self.gy = lax.axis_index("gy")
        self.gx = lax.axis_index("gx")

    def member(self, kind):
        if kind == "dp":
            return self.dp
        if kind == "y":
            return self.gx // 2
        if kind == "x":
            return self.gy // 2
        if kind == "z":
            return (self.gy % 2) * 2 + self.gx % 2
        if kind == "f":
            return self.dp * GX + self.gx
        return self.gy

    def device(self, kind, p):
        if kind == "dp":
            return (p, self.gy, self.gx)
        if kind == "y":
            return (self.dp, self.gy, p * 2 + self.gx % 2)
        if kind == "x":
            return (self.dp, p * 2 + self.gy % 2, self.gx)
        if kind == "z":
            return (self.dp, (self.gy // 2) * 2 + p // 2, (self.gx // 2) * 2 + p % 2)
        if kind == "f":
            return (p // GX, self.gy, p % GX)
        return (self.dp, p, self.gx)


SIZE = {"dp": 2, "y": 4, "x": 4, "z": 4, "f": 16, "g": 8}


class Reduce:
    def __init__(self, ring, rows, scatter, last, bufs, recvs, slots, out, send, recv, sent):
        self.ring = ring
        self.scatter = scatter
        self.last = last
        self.bufs = bufs
        self.recvs = recvs
        self.slots = slots
        self.out = out
        self.send = send
        self.recv = recv
        self.sent = sent
        self.used = 0
        self.rows = [rows]
        self.offs = [0]
        for kind in scatter:
            n = self.rows[-1] // SIZE[kind]
            self.offs.append(self.offs[-1] + ring.member(kind) * n)
            self.rows.append(n)

    def _go(self, src, dst, device):
        i = self.used
        self.used += 1
        c = pltpu.make_async_remote_copy(
            src_ref=src,
            dst_ref=dst,
            send_sem=self.send.at[i],
            recv_sem=self.recv.at[i],
            device_id=device,
            device_id_type=MESH,
        )
        c.start()
        self.sent.append(c)
        return c

    def scatter_start(self, s):
        kind, n = self.scatter[s], self.rows[s + 1]
        m, size = self.ring.member(kind), SIZE[kind]
        self.now = []
        for r in range(1, size):
            p = (m + r) % size
            src = self.bufs[s].at[pl.ds(pl.multiple_of(p * n, 16), n)]
            self.now.append(self._go(src, self.recvs[s].at[r - 1], self.ring.device(kind, p)))

    def scatter_end(self, s):
        kind, n = self.scatter[s], self.rows[s + 1]
        m, size = self.ring.member(kind), SIZE[kind]
        for c in self.now:
            c.wait_recv()
        total = self.bufs[s][pl.ds(pl.multiple_of(m * n, 16), n), :].astype(F32)
        for r in range(size - 1):
            total = total + self.recvs[s][r].astype(F32)
        total = total.astype(BF)
        if s + 1 < len(self.scatter):
            self.bufs[s + 1][...] = total
        else:
            self.slots[self.ring.member(self.last)] = total

    def last_start(self):
        m, size = self.ring.member(self.last), SIZE[self.last]
        self.now = []
        for r in range(1, size):
            p = (m + r) % size
            self.now.append(self._go(self.slots.at[m], self.slots.at[m], self.ring.device(self.last, p)))

    def last_end(self):
        for c in self.now:
            c.wait_recv()
        total = self.slots[0].astype(F32)
        for r in range(1, SIZE[self.last]):
            total = total + self.slots[r].astype(F32)
        self.out[pl.ds(pl.multiple_of(self.offs[-1], 16), self.rows[-1]), :] = total.astype(BF)

    def gather_start(self, s):
        kind, n = self.scatter[s], self.rows[s + 1]
        m, size = self.ring.member(kind), SIZE[kind]
        part = self.out.at[pl.ds(pl.multiple_of(self.offs[s + 1], 16), n)]
        self.now = []
        for r in range(1, size):
            p = (m + r) % size
            self.now.append(self._go(part, part, self.ring.device(kind, p)))

    def gather_end(self):
        for c in self.now:
            c.wait_recv()


def pack4(b):
    lane = lanes(b[0].shape)
    r1, r2, r3 = pltpu.roll(b[1], 96, 1), pltpu.roll(b[2], 64, 1), pltpu.roll(b[3], 32, 1)
    return (
        jnp.where(lane >= 96, r1, b[0]),
        jnp.where(lane < 64, r1, r2),
        jnp.where(lane < 32, r2, r3),
    )


def unpack4(d):
    lane = lanes(d[0].shape)
    return (
        d[0],
        pltpu.roll(jnp.where(lane >= 96, d[0], d[1]), 32, 1),
        pltpu.roll(jnp.where(lane >= 64, d[1], d[2]), 64, 1),
        pltpu.roll(d[2], 96, 1),
    )


def kernel(
    a_ref, wf_ref, we_ref, wm_ref, wl_ref, u_ref,
    mixed_ref, ig_ref, gf_ref, ge_ref, gm_ref, gl_ref,
    raw, pad2, pad3, e32, x3, x3t, fa, q, qet, qmt, c1, c2, ul, bl, gp, gfb, d32, mix32,
    wf, wft, we, wet, wm, wmt, wl, arm32, are32, arf32,
    sbuf, rbuf, h_send, h_recv,
    m0, m1, m2, mr0, mr1, mr2, mslot, mout, m_send, m_recv,
    e0, e1, e2, er0, er1, er2, eslot, eout, e_send, e_recv,
    f0, fr0, fslot, fout, f_send, f_recv,
):
    ring = Ring()
    dp, gy, gx = ring.dp, ring.gy, ring.gx

    barrier = pltpu.get_barrier_semaphore()
    met = 0
    for d in range(2):
        for x in range(GX):
            if (d, x) != (0, 0):
                pl.semaphore_signal(
                    barrier, inc=1, device_id=((dp + d) % 2, gy, (gx + x) % GX), device_id_type=MESH
                )
                met += 1
    for y in range(1, GY):
        for x in (-1, 0, 1) if y in (1, GY - 1) else (0,):
            pl.semaphore_signal(
                barrier, inc=1, device_id=(dp, (gy + y) % GY, (gx + x + GX) % GX), device_id_type=MESH
            )
            met += 1

    sent = []

    def edge(step, n):
        return {1: slice(n, n + 1), -1: slice(1, 2), 0: slice(1, n + 1)}[step]

    def outside(step, n):
        return {1: slice(0, 1), -1: slice(n + 1, n + 2), 0: slice(1, n + 1)}[step]

    def send_halo(ex, ref, n):
        copies = []
        for d, (dy, dx) in enumerate(DIRS):
            part = ref[edge(dy, n), edge(dx, n)].reshape(-1, L)
            if dy != 0 and dx != 0:
                part = jnp.concatenate([part, part], axis=0)
            rows = part.shape[0]
            sbuf[ex, d, 0:rows, :] = part.astype(BF)
            c = pltpu.make_async_remote_copy(
                src_ref=sbuf.at[ex, d, pl.ds(0, rows)],
                dst_ref=rbuf.at[ex, d, pl.ds(0, rows)],
                send_sem=h_send.at[ex * 8 + d],
                recv_sem=h_recv.at[ex * 8 + d],
                device_id=(dp, (gy + dy + GY) % GY, (gx + dx + GX) % GX),
                device_id_type=MESH,
            )
            c.start()
            sent.append(c)
            copies.append(c)
        return copies

    def take_halo(ex, ref, n, copies):
        for d, (dy, dx) in enumerate(DIRS):
            copies[d].wait_recv()
            there = jnp.logical_and(
                jnp.logical_and(gy - dy >= 0, gy - dy < GY),
                jnp.logical_and(gx - dx >= 0, gx - dx < GX),
            )
            keep = jnp.where(there, 1.0, 0.0).astype(F32)
            ys, xs = outside(dy, n), outside(dx, n)
            ny, nx = ys.stop - ys.start, xs.stop - xs.start
            part = rbuf[ex, d, 0 : max(ny * nx * Z, 16), :].astype(F32)[: ny * nx * Z]
            ref[ys, xs] = (part * keep).reshape(ny, nx, Z, L)

    def read_cells(src_ref, dst, shift):
        for t in range(TILES):
            raw[t] = src_ref[0, :, :, t * L : (t + 1) * L].astype(F32).reshape(Z * N2, L)

        def row(y, _):
            tiles = [raw[t, pl.ds(y, Z, stride=N2), :] for t in range(TILES)]
            lane = lanes((Z, L))
            for x in range(N2):
                t, o = (x * C2) // L, (x * C2) % L
                cell = tiles[t] if o == 0 else pltpu.roll(tiles[t], L - o, 1)
                if o + C2 > L:
                    cell = jnp.where(lane < L - o, cell, pltpu.roll(tiles[t + 1], L - o, 1))
                dst[y + shift, x + shift] = jnp.where(lane < C2, cell, 0.0)
            return 0

        lax.fori_loop(0, N2, row, 0)

    def write_cells(src, out32, dst_ref):
        def row(y, _):
            tiles = [None] * TILES
            lane = lanes((Z, L))
            for x in range(N2):
                t, o = (x * C2) // L, (x * C2) % L
                cell = src[y, x]
                cell = cell if o == 0 else pltpu.roll(cell, o, 1)
                tiles[t] = cell if o == 0 else jnp.where(lane >= o, cell, tiles[t])
                if o + C2 > L:
                    tiles[t + 1] = cell
            for t in range(TILES):
                out32[t, pl.ds(y, Z, stride=N2), :] = tiles[t]
            return 0

        lax.fori_loop(0, N2, row, 0)
        for t in range(TILES):
            dst_ref[0, :, :, t * L : (t + 1) * L] = out32[t].reshape(Z, N2, L).astype(BF)

    def fine_columns():
        def row(y, _):
            for k in range(3):
                x3[y, :, k * L : (k + 1) * L] = pad2[y, k : k + N2].reshape(N2 * Z, L).astype(BF)
            return 0

        lax.fori_loop(0, N2 + 2, row, 0)

    def fine_rows(chunk):
        parts = [x3[pl.ds(chunk * 4 + j, 4)].reshape(4 * N2 * Z, 3 * L) for j in range(3)]
        return jnp.concatenate(parts, axis=1)

    def coarse_columns():
        for j in range(3):
            for k in range(3):
                t = j * 3 + k
                q[:, t * L : (t + 1) * L] = (
                    pad3[j : j + N3, k : k + N3].reshape(N3 * N3 * Z, L).astype(BF)
                )

    def joined(acc):
        acc = acc.reshape(N3 * N3, Z, 3 * L)
        return shift_z(acc[:, :, 0:L], 1) + acc[:, :, L : 2 * L] + shift_z(acc[:, :, 2 * L :], -1)

    def put3(v):
        pad3[1 : N3 + 1, 1 : N3 + 1] = v.reshape(N3, N3, Z, L)

    def coarse_weight_grad(qt, g):
        g3 = jnp.concatenate([shift_z(g, -1), g, shift_z(g, 1)], axis=2)
        g3 = g3.reshape(N3 * N3 * Z, 3 * L).astype(BF)
        return nn(qt[...], g3).reshape(9, L, 3 * L)

    read_cells(a_ref, pad2, 1)
    pl.semaphore_wait(barrier, met)
    copies = send_halo(EX_IN, pad2, N2)

    for ref in (wf, wft, we, wet, wm, wmt, wl):
        ref[...] = jnp.zeros(ref.shape, BF)
    wl[0:C3, 0:C2] = wl_ref[...]
    for j in range(3):
        for k in range(3):
            t = (j * 3 + k) * L
            wf[t : t + C2, 0:C2] = wf_ref[j, k]
            wft[0:C2, t : t + C2] = wf_ref[2 - j, 2 - k]
            for i in range(3):
                we[t : t + C2, i * L : i * L + C3] = we_ref[i, j, k]
                wm[t : t + C3, i * L : i * L + C3] = wm_ref[i, j, k]
                wet[i * L : i * L + C2, t : t + C3] = we_ref[2 - i, 2 - j, 2 - k]
                wmt[i * L : i * L + C3, t : t + C3] = wm_ref[2 - i, 2 - j, 2 - k]
    read_cells(u_ref, e32, 0)
    low = e32[...].reshape(N3, 2, N3, 2, Z, L)
    low = (low[:, 0, :, 0] + low[:, 0, :, 1]) + (low[:, 1, :, 0] + low[:, 1, :, 1])
    ul[...] = low.reshape(N3 * N3 * Z, L).astype(BF)
    bl[...] = nt(ul[...], wl[...])

    take_halo(EX_IN, pad2, N2, copies)
    fine_columns()

    def fine_forward(chunk, _):
        act = elu(nn(fine_rows(chunk), wf[...])).astype(BF)
        fa[pl.ds(chunk * 4, 4)] = act.reshape(4, N2 * Z, L)
        v = act.astype(F32).reshape(2, 2, N3, 2, Z, L)
        v = (v[:, 0, :, 0] + v[:, 0, :, 1]) + (v[:, 1, :, 0] + v[:, 1, :, 1])
        pad3[pl.ds(chunk * 2 + 1, 2), 1 : N3 + 1] = rounded(0.25 * v)
        return 0

    lax.fori_loop(0, 4, fine_forward, 0)
    copies = send_halo(EX_POOL, pad3, N3)

    def turn(y, _):
        x3t[:, pl.ds(pl.multiple_of(y * L, L), L)] = x3[y].T
        return 0

    lax.fori_loop(0, N2 + 2, turn, 0)

    take_halo(EX_POOL, pad3, N3, copies)
    coarse_columns()
    c1[...] = rounded(elu(joined(nn(q[...], we[...]))))
    put3(c1[...])
    copies = send_halo(EX_ONE, pad3, N3)
    qet[...] = q[...].T

    take_halo(EX_ONE, pad3, N3, copies)
    coarse_columns()
    two = rounded(elu(joined(nn(q[...], wm[...]))))
    c2[...] = two
    g2 = rounded(bl[...].reshape(N3 * N3, Z, L) * slope(two))
    put3(g2)
    copies = send_halo(EX_G2, pad3, N3)

    qmt[...] = q[...].T
    mid = coarse_weight_grad(qmt, pad3[1 : N3 + 1, 1 : N3 + 1].reshape(N3 * N3, Z, L))
    two = c2[...].reshape(N3 * N3 * Z, L).astype(BF)
    lift_grad = nn(two.T, ul[...])
    blocks = [mid[t, :C3, i * L : (i + 1) * L] for i in range(3) for t in range(9)]
    blocks.append(lift_grad[:C3])
    for g in range(7):
        for d, part in enumerate(pack4(blocks[4 * g : 4 * g + 4])):
            m0[(g * 3 + d) * C3 : (g * 3 + d + 1) * C3, :] = part.astype(BF)
    m0[21 * C3 :, :] = jnp.zeros((ROWS_M - 21 * C3, L), BF)
    red_m = Reduce(
        ring, ROWS_M, ("dp", "y", "x"), "z", (m0, m1, m2), (mr0, mr1, mr2), mslot, mout, m_send, m_recv, sent
    )
    red_m.scatter_start(0)

    take_halo(EX_G2, pad3, N3, copies)
    coarse_columns()
    g1 = rounded(joined(nt(q[...], wmt[...])) * slope(c1[...]))
    put3(g1)
    copies = send_halo(EX_G1, pad3, N3)

    red_m.scatter_end(0)
    red_m.scatter_start(1)
    ent = coarse_weight_grad(qet, pad3[1 : N3 + 1, 1 : N3 + 1].reshape(N3 * N3, Z, L))
    blocks = [ent[t, :C2, i * L : (i + 1) * L] for i in range(3) for t in range(9)]
    blocks.append(jnp.zeros((C2, L), F32))
    for g in range(7):
        for d, part in enumerate(pack4(blocks[4 * g : 4 * g + 4])):
            are32[(g * 3 + d) * C2 : (g * 3 + d + 1) * C2, :] = part
    are32[21 * C2 :, :] = jnp.zeros((ROWS_E - 21 * C2, L), F32)
    e0[...] = are32[...].astype(BF)
    red_e = Reduce(
        ring, ROWS_E, ("dp", "x", "y"), "z", (e0, e1, e2), (er0, er1, er2), eslot, eout, e_send, e_recv, sent
    )
    red_e.scatter_start(0)

    take_halo(EX_G1, pad3, N3, copies)
    coarse_columns()
    gp[...] = 0.25 * rounded(joined(nt(q[...], wet[...]))).reshape(N3, N3, Z, L)

    def fine_back(y, _):
        act = fa[pl.ds(y * 2, 2)].astype(F32).reshape(2, N3, 2, Z, L)
        e = e32[pl.ds(y * 2, 2)].reshape(2, N3, 2, Z, L)
        up = gp[pl.ds(y, 1)].reshape(1, N3, 1, Z, L)
        g = ((e + up) * slope(act)).reshape(2, N2, Z, L).astype(BF)
        gfb[pl.ds(pl.multiple_of(y * 2 * L, 2 * L), 2 * L), :] = g.reshape(2 * N2 * Z, L)
        pad2[pl.ds(y * 2 + 1, 2), 1 : N2 + 1] = g.astype(F32)
        return 0

    lax.fori_loop(0, N3, fine_back, 0)
    copies = send_halo(EX_FINE, pad2, N2)

    for j in range(3):
        grad = nn(x3t[:, j * L : (j + N2) * L], gfb[...])
        b0, b1, b2 = grad[0:C2], grad[L : L + C2], grad[2 * L : 2 * L + C2]
        lane = lanes(b0.shape)
        r1, r2 = pltpu.roll(b1, C2, 1), pltpu.roll(b2, 2 * C2 - L, 1)
        arf32[2 * j * C2 : (2 * j + 1) * C2, :] = jnp.where(lane < C2, b0, r1)
        arf32[(2 * j + 1) * C2 : (2 * j + 2) * C2, :] = jnp.where(lane < 2 * C2 - L, r1, r2)
    arf32[6 * C2 :, :] = jnp.zeros((ROWS_F - 6 * C2, L), F32)
    f0[...] = arf32[...].astype(BF)
    red_f = Reduce(ring, ROWS_F, ("f",), "g", (f0,), (fr0,), fslot, fout, f_send, f_recv, sent)
    red_f.scatter_start(0)
    red_m.scatter_end(1)
    red_m.scatter_start(2)
    red_e.scatter_end(0)
    red_e.scatter_start(1)

    two = c2[...].reshape(N3 * N3 * Z, L).astype(BF)
    gp[...] = rounded(nn(two, wl[...])).reshape(N3, N3, Z, L)

    def mix(y, _):
        act = fa[pl.ds(y * 2, 2)].astype(F32).reshape(2, N3, 2, Z, L)
        up = gp[pl.ds(y, 1)].reshape(1, N3, 1, Z, L)
        d32[pl.ds(y * 2, 2)] = (act + up).reshape(2, N2, Z, L)
        return 0

    lax.fori_loop(0, N3, mix, 0)
    write_cells(d32, mix32, mixed_ref)

    red_f.scatter_end(0)
    red_f.last_start()
    red_m.scatter_end(2)
    red_m.last_start()
    red_e.scatter_end(1)
    red_e.scatter_start(2)

    take_halo(EX_FINE, pad2, N2, copies)
    fine_columns()

    def fine_backward(chunk, _):
        d32[pl.ds(chunk * 4, 4)] = nt(fine_rows(chunk), wft[...]).reshape(4, N2, Z, L)
        return 0

    lax.fori_loop(0, 4, fine_backward, 0)

    red_f.last_end()
    red_f.gather_start(0)
    red_m.last_end()
    red_m.gather_start(2)
    red_e.scatter_end(2)
    red_e.last_start()

    write_cells(d32, raw, ig_ref)

    red_m.gather_end()
    red_m.gather_start(1)
    red_e.last_end()
    red_e.gather_start(2)

    red_f.gather_end()
    arf32[...] = fout[...].astype(F32)
    for j in range(3):
        d0 = arf32[2 * j * C2 : (2 * j + 1) * C2, :]
        d1 = arf32[(2 * j + 1) * C2 : (2 * j + 2) * C2, :]
        lane = lanes(d0.shape)
        b1 = pltpu.roll(jnp.where(lane >= C2, d0, d1), L - C2, 1)
        b2 = pltpu.roll(d1, 2 * L - 2 * C2, 1)
        for k, b in enumerate((d0, b1, b2)):
            gf_ref[j, k] = b[:, 0:C2]

    red_e.gather_end()
    red_e.gather_start(1)
    red_m.gather_end()
    red_m.gather_start(0)
    red_e.gather_end()
    red_e.gather_start(0)

    red_m.gather_end()
    for g in range(7):
        d = [mout[(g * 3 + s) * C3 : (g * 3 + s + 1) * C3, :].astype(F32) for s in range(3)]
        for s, b in enumerate(unpack4(d)):
            t = g * 4 + s
            if t < 27:
                gm_ref[t // 9, (t // 3) % 3, t % 3] = b[:, 0:C3]
            else:
                gl_ref[...] = b[:, 0:C2]

    red_e.gather_end()
    are32[...] = eout[...].astype(F32)
    for g in range(7):
        d = [are32[(g * 3 + s) * C2 : (g * 3 + s + 1) * C2, :] for s in range(3)]
        for s, b in enumerate(unpack4(d)):
            t = g * 4 + s
            if t < 27:
                ge_ref[t // 9, (t // 3) % 3, t % 3] = b[:, 0:C3]

    for c in sent:
        c.wait_send()


def body(fine_input, fine_weight, entry_weight, middle_weight, lift_weight, upstream):
    field = jax.ShapeDtypeStruct(fine_input.shape, BF)
    vmem = pl.BlockSpec(memory_space=pltpu.VMEM)
    cells2, cells3 = N2 * N2 * Z, N3 * N3 * Z

    def v(*shape, dtype=BF):
        return pltpu.VMEM(shape, dtype)

    def w(*shape):
        return pltpu.VMEM(shape, F32)

    def sems(n):
        return [pltpu.SemaphoreType.DMA((n,)), pltpu.SemaphoreType.DMA((n,))]

    m, e, f = ROWS_M, ROWS_E, ROWS_F
    scratch = [
        w(TILES, Z * N2, L), w(N2 + 2, N2 + 2, Z, L), w(N3 + 2, N3 + 2, Z, L), w(N2, N2, Z, L),
        v(N2 + 2, N2 * Z, 3 * L), v(3 * L, (N2 + 2) * N2 * Z), v(N2, N2 * Z, L),
        v(cells3, 9 * L), v(9 * L, cells3), v(9 * L, cells3),
        w(N3 * N3, Z, L), w(N3 * N3, Z, L), v(cells3, L), w(cells3, L), w(N3, N3, Z, L),
        v(cells2, L), w(N2, N2, Z, L), w(TILES, Z * N2, L),
        v(9 * L, L), v(L, 9 * L), v(9 * L, 3 * L), v(3 * L, 9 * L), v(9 * L, 3 * L), v(3 * L, 9 * L), v(L, L),
        w(8, L), w(e, L), w(f, L),
        v(6, 8, N2 * Z, L), v(6, 8, N2 * Z, L), *sems(48),
        v(m, L), v(m // 2, L), v(m // 8, L),
        v(1, m // 2, L), v(3, m // 8, L), v(3, m // 32, L), v(4, m // 32, L), v(m, L), *sems(17),
        v(e, L), v(e // 2, L), v(e // 8, L),
        v(1, e // 2, L), v(3, e // 8, L), v(3, e // 32, L), v(4, e // 32, L), v(e, L), *sems(17),
        v(f, L), v(15, f // 16, L), v(8, f // 16, L), v(f, L), *sems(37),
    ]
    return pl.pallas_call(
        kernel,
        out_shape=(
            field,
            field,
            jax.ShapeDtypeStruct(fine_weight.shape, F32),
            jax.ShapeDtypeStruct(entry_weight.shape, F32),
            jax.ShapeDtypeStruct(middle_weight.shape, F32),
            jax.ShapeDtypeStruct(lift_weight.shape, F32),
        ),
        in_specs=[vmem] * 6,
        out_specs=[vmem] * 6,
        scratch_shapes=scratch,
        compiler_params=pltpu.CompilerParams(
            collective_id=0, has_side_effects=True, vmem_limit_bytes=60 * 1024 * 1024
        ),
    )(fine_input, fine_weight, entry_weight, middle_weight, lift_weight, upstream)


def solution(mesh):
    assert mesh.shape["gy"] == GY and mesh.shape["gx"] == GX
    return jax.shard_map(
        body,
        mesh=mesh,
        in_specs=(P("dp", None, "gy", "gx"), P(), P(), P(), P(), P("dp", None, "gy", "gx")),
        out_specs=(P("dp", None, "gy", "gx"), P("dp", None, "gy", "gx"), P(), P(), P(), P()),
        check_vma=False,
    )
```

time: 494 us -> 85.4 us (0.17); the launches traced: 484 us -> 85.1 us
  waiting for transfers between devices: 161 us -> 0 us
  local copies, waits for them, and re-layouts: 96.1 us -> 10.2 us
  blocking collectives: 76.7 us -> 0 us
  Pallas kernels: 0 us -> 74.2 us
  starting transfers between devices: 66.7 us -> 0 us
  other arithmetic: 36.1 us -> 0 us
  matrix products: 31 us -> 0 us
  between operations: 16.3 us -> 0.65 us
    psum x1 -> x0, waiting for transfers between devices: 143 us -> none  [body(): lax.psum((fine_grad, entry_grad, middle_grad, lift_grad), ('dp', 'gy', 'g...]
    psum x1 -> x0, blocking collectives: 76.7 us -> none  [body(): lax.psum((fine_grad, entry_grad, middle_grad, lift_grad), ('dp', 'gy', 'g...]
    pallas_call x0 -> x1, Pallas kernels: none -> 74.2 us  [body(): pl.pallas_call(kernel, out_shape=(field, field, jax.ShapeDtypeStruct(fine...]
    ppermute x24 -> x0, starting transfers between devices: 66.7 us -> none  [the longest x12 50.5 us: padded_2(): lax.ppermute(lax.slice_in_dim(block, block.shape[dim] - width, None, axis...]
    dot_general x66 -> x0, matrix products: 31 us -> none  [the longest x42 16.2 us: conv_taps(): jnp.dot(stacked.reshape(-1, 3 * channels), weight[z_tap, y_tap].reshape(3...]
    slice x38 -> x0, local copies, waits for them, and re-layouts: 24.2 us -> none  [the longest x18 13.5 us: conv_taps(): weight[z_tap, y_tap].reshape(3 * channels, outputs)]
    concatenate x38 -> x0, other arithmetic: 18.9 us -> none  [the longest x28 14.3 us: conv_taps(): jnp.concatenate([padded[:, z_tap:z_tap + depth, y_tap:y_tap + row_count,...]
    dot_general x20 -> x0, local copies, waits for them, and re-layouts: 18.9 us -> none  [weight_grad(): lax.dot_general(stacked.reshape(-1, 3 * channels), flattened, (((0,), (0,...]
  transfers between devices with their start and end apart: 25 -> 0, of which waited for: 8 -> 0; matrix products, arithmetic and copies ran while one was open for 17% -> 0% of each run, Pallas kernels for 0% -> 0%
where the time goes in v1:
time: 85.4 us; the launch traced here: 85.1 us
  Pallas kernels  74.2 us (87%)
  local copies, waits for them, and re-layouts  10.2 us (12%)
    pallas_call x1, Pallas kernels, body(): pl.pallas_call(kernel, out_shape=(field, field, jax.ShapeDtypeStruct(fine...  74.2 us
    unnamed x10, local copies, waits for them, and re-layouts  8.66 us

profile of v1, /device:TPU:1, one launch (start us, length us, event | category | flops | bytes accessed | tf_op | source)
XLA Modules:
  0.0 85.1 jit_solution(6554922043803902088)
XLA Ops:
  0.6 1.4 %copy.12.wl_ref = bf16[96,72]{1,0:T(8,128)(2,1)} copy(bf16[96,72]{0,1:T(8,128)(2,1)} %param.10) | data formatting | bytes 27648 | tf_op args[4]
  2.1 74.2 %shard_map.109 = (bf16[1,8,16,1152]{3,2,1,0:T(8,128)(2,1)}, bf16[1,8,16,1152]{3,2,1,0:T(8,128)(2,1)}, f32[3,3,72,72]{3,2,1,0:T(8,128)}, f32[3,3,3,72,96]{4,3,2,1...) custom-call(bf16[1,8,16,1152]{3,2,1,0:T(8,128)(2,1)} %a_ref.1, bf16[3,3,72,72]{3,2,1,0:T(8,128)(2,1)} %wf_ref.1, ...), custom_call_target="tpu_custom_call" | custom-call | tf_op jit(solution)/shard_map/pallas_call | solution.py:584
  76.3 0.0 copy-start.1
  76.3 1.6 %copy.13 = f32[96,72]{0,1:T(8,128)} copy(f32[96,72]{1,0:T(8,128)} %get-tuple-element.11) | data formatting | bytes 55296 | tf_op jit(solution)/shard_map/pallas_call | solution.py:584
  77.9 1.7 %copy.19 = bf16[1,8,16,1152]{3,2,1,0:T(8,128)(2,1)} copy(bf16[1,8,16,1152]{3,2,1,0:T(8,128)(2,1)} %get-tuple-element.18) | data formatting | bytes 589824
  79.6 1.7 %copy.20 = bf16[1,8,16,1152]{3,2,1,0:T(8,128)(2,1)} copy(bf16[1,8,16,1152]{3,2,1,0:T(8,128)(2,1)} %get-tuple-element.19) | data formatting | bytes 589824
  81.3 0.0 copy-start
  81.3 1.8 %copy.21 = f32[3,3,72,72]{3,2,1,0:T(8,128)} copy(f32[3,3,72,72]{3,2,1,0:T(8,128)} %get-tuple-element.20) | data formatting | bytes 373248
  83.1 0.0 copy-done.1
  83.1 0.9 %copy.22 = f32[3,3,3,72,96]{4,3,2,1,0:T(8,128)} copy(f32[3,3,3,72,96]{4,3,2,1,0:T(8,128)S(1)} %copy-done.1) | data formatting | bytes 1492992
  84.0 0.0 copy-done
  84.0 1.1 %copy.23 = f32[3,3,3,96,96]{4,3,2,1,0:T(8,128)} copy(f32[3,3,3,96,96]{4,3,2,1,0:T(8,128)S(1)} %copy-done) | data formatting | bytes 1990656
Async XLA Ops:
  76.3 6.8 %copy-start.1 = (f32[3,3,3,72,96]{4,3,2,1,0:T(8,128)S(1)}, f32[3,3,3,72,96]{4,3,2,1,0:T(8,128)}, u32[]{:S(2)}) copy-start(f32[3,3,3,72,96]{4,3,2,1,0:T(8,128)} %get-tuple-element.21) | copy-start | bytes 2239492
  81.3 2.8 %copy-start = (f32[3,3,3,96,96]{4,3,2,1,0:T(8,128)S(1)}, f32[3,3,3,96,96]{4,3,2,1,0:T(8,128)}, u32[]{:S(2)}) copy-start(f32[3,3,3,96,96]{4,3,2,1,0:T(8,128)} %get-tuple-element.22) | copy-start | bytes 2985988

commit v2 on v1

v2 whole, which is shorter than its diff:
```python
import jax
import jax.numpy as jnp
from jax import lax
from jax.experimental import pallas as pl
from jax.experimental.pallas import tpu as pltpu
from jax.sharding import PartitionSpec as P

MESH = pl.DeviceIdType.MESH
BF = jnp.bfloat16
F32 = jnp.float32

Z = 8
N2 = 16
N3 = 8
C2 = 72
C3 = 96
L = 128
GY = 8
GX = 8
MERGED = N2 * C2
TILES = MERGED // L
DIRS = [(dy, dx) for dy in (-1, 0, 1) for dx in (-1, 0, 1) if (dy, dx) != (0, 0)]

EX_IN, EX_POOL, EX_LOW, EX_G1, EX_FINE = range(5)

ROWS_M = 2048
ROWS_E = 1536
ROWS_F = 512


def lanes(shape):
    return lax.broadcasted_iota(jnp.int32, shape, len(shape) - 1)


def elu(v):
    return jnp.where(v > 0, v, jnp.exp(jnp.minimum(v, 0.0)) - 1.0)


def slope(s):
    return jnp.where(s > 0, 1.0, 1.0 + s)


def rounded(v):
    return v.astype(BF).astype(F32)


def shift_z(v, step):
    moved = pltpu.roll(v, step % Z, 1)
    row = lax.broadcasted_iota(jnp.int32, v.shape, 1)
    return jnp.where(row == (0 if step == 1 else Z - 1), 0.0, moved)


def nt(a, b):
    return lax.dot_general(a, b, (((1,), (1,)), ((), ())), preferred_element_type=F32)


def tn(a, b):
    return lax.dot_general(a, b, (((0,), (0,)), ((), ())), preferred_element_type=F32)


def nn(a, b):
    return jnp.dot(a, b, preferred_element_type=F32)


class Ring:
    def __init__(self):
        self.dp = lax.axis_index("dp")
        self.gy = lax.axis_index("gy")
        self.gx = lax.axis_index("gx")

    def member(self, kind):
        if kind == "dp":
            return self.dp
        if kind == "xy":
            return (self.gy // 2) * 4 + self.gx // 2
        return (self.gy % 2) * 2 + self.gx % 2

    def device(self, kind, p):
        if kind == "dp":
            return (p, self.gy, self.gx)
        if kind == "xy":
            return (self.dp, (p // 4) * 2 + self.gy % 2, (p % 4) * 2 + self.gx % 2)
        return (self.dp, (self.gy // 2) * 2 + p // 2, (self.gx // 2) * 2 + p % 2)

    def others(self, kind):
        m = self.member(kind)
        if kind == "dp":
            return [1 - m]
        if kind == "z":
            return [(m + r) % 4 for r in (2, 1, 3)]
        steps = [(2, 2), (2, 1), (1, 2), (2, 3), (3, 2), (1, 1), (1, 3), (3, 1), (3, 3)]
        steps += [(2, 0), (0, 2), (1, 0), (0, 1), (3, 0), (0, 3)]
        return [((m // 4 + x) % 4) * 4 + (m % 4 + y) % 4 for x, y in steps]


SIZE = {"dp": 2, "xy": 16, "z": 4}


class Reduce:
    scatter = ("dp", "xy")
    last = "z"

    def __init__(self, ring, rows, bufs, recvs, slots, out, send, recv, sent):
        self.ring = ring
        self.bufs = bufs
        self.recvs = recvs
        self.slots = slots
        self.out = out
        self.send = send
        self.recv = recv
        self.sent = sent
        self.used = 0
        self.rows = [rows]
        self.offs = [0]
        for kind in self.scatter:
            n = self.rows[-1] // SIZE[kind]
            self.offs.append(self.offs[-1] + ring.member(kind) * n)
            self.rows.append(n)

    def _go(self, src, dst, device):
        i = self.used
        self.used += 1
        c = pltpu.make_async_remote_copy(
            src_ref=src,
            dst_ref=dst,
            send_sem=self.send.at[i],
            recv_sem=self.recv.at[i],
            device_id=device,
            device_id_type=MESH,
        )
        c.start()
        self.sent.append(c)
        return c

    def scatter_start(self, s):
        kind, n = self.scatter[s], self.rows[s + 1]
        self.now = []
        for r, p in enumerate(self.ring.others(kind)):
            src = self.bufs[s].at[pl.ds(pl.multiple_of(p * n, 16), n)]
            self.now.append(self._go(src, self.recvs[s].at[r], self.ring.device(kind, p)))

    def scatter_end(self, s):
        kind, n = self.scatter[s], self.rows[s + 1]
        m, size = self.ring.member(kind), SIZE[kind]
        for c in self.now:
            c.wait_recv()
        total = self.bufs[s][pl.ds(pl.multiple_of(m * n, 16), n), :].astype(F32)
        for r in range(size - 1):
            total = total + self.recvs[s][r].astype(F32)
        total = total.astype(BF)
        if s + 1 < len(self.scatter):
            self.bufs[s + 1][...] = total
        else:
            self.slots[self.ring.member(self.last)] = total

    def last_start(self):
        m = self.ring.member(self.last)
        self.now = []
        for p in self.ring.others(self.last):
            self.now.append(self._go(self.slots.at[m], self.slots.at[m], self.ring.device(self.last, p)))

    def last_end(self):
        for c in self.now:
            c.wait_recv()
        total = self.slots[0].astype(F32)
        for r in range(1, SIZE[self.last]):
            total = total + self.slots[r].astype(F32)
        self.out[pl.ds(pl.multiple_of(self.offs[-1], 16), self.rows[-1]), :] = total.astype(BF)

    def gather_start(self, s):
        kind, n = self.scatter[s], self.rows[s + 1]
        part = self.out.at[pl.ds(pl.multiple_of(self.offs[s + 1], 16), n)]
        self.now = []
        for p in self.ring.others(kind):
            self.now.append(self._go(part, part, self.ring.device(kind, p)))

    def gather_end(self):
        for c in self.now:
            c.wait_recv()


def pack4(b):
    lane = lanes(b[0].shape)
    r1, r2, r3 = pltpu.roll(b[1], 96, 1), pltpu.roll(b[2], 64, 1), pltpu.roll(b[3], 32, 1)
    return (
        jnp.where(lane >= 96, r1, b[0]),
        jnp.where(lane < 64, r1, r2),
        jnp.where(lane < 32, r2, r3),
    )


def unpack4(d):
    lane = lanes(d[0].shape)
    return (
        d[0],
        pltpu.roll(jnp.where(lane >= 96, d[0], d[1]), 32, 1),
        pltpu.roll(jnp.where(lane >= 64, d[1], d[2]), 64, 1),
        pltpu.roll(d[2], 96, 1),
    )


def kernel(
    a_hbm, wf_hbm, we_hbm, wm_hbm, wl_hbm, u_hbm,
    mixed_hbm, ig_hbm, mout, eout, fout,
    a_ref, wf_ref, we_ref, wm_ref, wl_ref, u_ref, mixed_ref, ig_ref, in_sem, out_sem,
    raw, raw2, pad2, pad3, ulp, e32, x3, g3f, fa, q, c1p, c2, gp, gup, d32,
    wf, wft, we, wet, wm, wmt, wl, are32, arf32,
    sbuf, rbuf, h_send, h_recv,
    m0, m1, mr0, mr1, mslot, m_send, m_recv,
    e0, e1, er0, er1, eslot, e_send, e_recv,
    f0, f1, fr0, fr1, fslot, f_send, f_recv,
):
    ring = Ring()
    dp, gy, gx = ring.dp, ring.gy, ring.gx

    barrier = pltpu.get_barrier_semaphore()
    met = [(dp, (gy + dy + GY) % GY, (gx + dx + GX) % GX) for dy, dx in DIRS]
    met += [ring.device(kind, p) for kind in ("dp", "xy") for p in ring.others(kind)]
    for device in met:
        pl.semaphore_signal(barrier, inc=1, device_id=device, device_id_type=MESH)

    loads = [
        pltpu.make_async_copy(src, dst, in_sem.at[i])
        for i, (src, dst) in enumerate(
            (
                (a_hbm, a_ref), (u_hbm, u_ref), (wf_hbm, wf_ref),
                (we_hbm, we_ref), (wm_hbm, wm_ref), (wl_hbm, wl_ref),
            )
        )
    ]
    for c in loads:
        c.start()

    sent = []

    def edge(step, n, w):
        return {1: slice(n, n + w), -1: slice(w, 2 * w), 0: slice(w, n + w)}[step]

    def outside(step, n, w):
        return {1: slice(0, w), -1: slice(n + w, n + 2 * w), 0: slice(w, n + w)}[step]

    def send_halo(ex, ref, n, w):
        copies = []
        for d, (dy, dx) in enumerate(DIRS):
            part = ref[edge(dy, n, w), edge(dx, n, w)].reshape(-1, L)
            if part.shape[0] % 16:
                part = jnp.concatenate([part, part[:Z]], axis=0)
            rows = part.shape[0]
            sbuf[ex, d, 0:rows, :] = part.astype(BF)
            c = pltpu.make_async_remote_copy(
                src_ref=sbuf.at[ex, d, pl.ds(0, rows)],
                dst_ref=rbuf.at[ex, d, pl.ds(0, rows)],
                send_sem=h_send.at[ex * 8 + d],
                recv_sem=h_recv.at[ex * 8 + d],
                device_id=(dp, (gy + dy + GY) % GY, (gx + dx + GX) % GX),
                device_id_type=MESH,
            )
            c.start()
            sent.append(c)
            copies.append(c)
        return copies

    def take_halo(ex, ref, n, w, copies):
        for d, (dy, dx) in enumerate(DIRS):
            copies[d].wait_recv()
            there = jnp.logical_and(
                jnp.logical_and(gy - dy >= 0, gy - dy < GY),
                jnp.logical_and(gx - dx >= 0, gx - dx < GX),
            )
            keep = jnp.where(there, 1.0, 0.0).astype(F32)
            ys, xs = outside(dy, n, w), outside(dx, n, w)
            ny, nx = ys.stop - ys.start, xs.stop - xs.start
            part = rbuf[ex, d, 0 : max(ny * nx * Z, 16), :].astype(F32)[: ny * nx * Z]
            ref[ys, xs] = (part * keep).reshape(ny, nx, Z, L)

    def spread(src_ref):
        for t in range(TILES):
            raw[t] = src_ref[0, :, :, t * L : (t + 1) * L].astype(F32).reshape(Z * N2, L)

    def read_row(y, xs, dst, shift):
        lane = lanes((Z, L))
        tiles = {}
        for x in xs:
            t, o = (x * C2) // L, (x * C2) % L
            for s in (t, t + 1) if o + C2 > L else (t,):
                if s not in tiles:
                    tiles[s] = raw[s, pl.ds(y, Z, stride=N2), :]
            cell = tiles[t] if o == 0 else pltpu.roll(tiles[t], L - o, 1)
            if o + C2 > L:
                cell = jnp.where(lane < L - o, cell, pltpu.roll(tiles[t + 1], L - o, 1))
            dst[y + shift, x + shift] = jnp.where(lane < C2, cell, 0.0)

    def read_rows(first, last, xs, dst, shift):
        def row(y, _):
            read_row(y, xs, dst, shift)
            return 0

        lax.fori_loop(first, last, row, 0)

    def write_cells(src, out32, dst_ref):
        def row(y, _):
            tiles = [None] * TILES
            lane = lanes((Z, L))
            for x in range(N2):
                t, o = (x * C2) // L, (x * C2) % L
                cell = src[y, x]
                cell = cell if o == 0 else pltpu.roll(cell, o, 1)
                tiles[t] = cell if o == 0 else jnp.where(lane >= o, cell, tiles[t])
                if o + C2 > L:
                    tiles[t + 1] = cell
            for t in range(TILES):
                out32[t, pl.ds(y, Z, stride=N2), :] = tiles[t]
            return 0

        lax.fori_loop(0, N2, row, 0)
        for t in range(TILES):
            dst_ref[0, :, :, t * L : (t + 1) * L] = out32[t].reshape(Z, N2, L).astype(BF)

    def fine_columns():
        def row(y, _):
            for k in range(3):
                x3[y, :, k * L : (k + 1) * L] = pad2[y, k : k + N2].reshape(N2 * Z, L).astype(BF)
            return 0

        lax.fori_loop(0, N2 + 2, row, 0)

    def fine_rows(chunk):
        parts = [x3[pl.ds(chunk * 4 + j, 4)].reshape(4 * N2 * Z, 3 * L) for j in range(3)]
        return jnp.concatenate(parts, axis=1)

    def columns(ref, n, off=0):
        rows = n * n * Z
        for j in range(3):
            for k in range(3):
                t = (j * 3 + k) * L
                q[0:rows, t : t + L] = (
                    ref[off + j : off + j + n, off + k : off + k + n].reshape(rows, L).astype(BF)
                )
        return q[0:rows, :]

    def joined(acc):
        acc = acc.reshape(-1, Z, 3 * L)
        return shift_z(acc[:, :, 0:L], 1) + acc[:, :, L : 2 * L] + shift_z(acc[:, :, 2 * L :], -1)

    def coarse_weight_grad(taps, g):
        g3 = jnp.concatenate([shift_z(g, -1), g, shift_z(g, 1)], axis=2)
        g3 = g3.reshape(N3 * N3 * Z, 3 * L).astype(BF)
        return tn(taps, g3).reshape(9, L, 3 * L)

    loads[0].wait()
    spread(a_ref)
    read_row(0, range(N2), pad2, 1)
    read_row(N2 - 1, range(N2), pad2, 1)
    read_rows(1, N2 - 1, (0, N2 - 1), pad2, 1)
    pl.semaphore_wait(barrier, len(met))
    copies = send_halo(EX_IN, pad2, N2, 1)

    read_rows(1, N2 - 1, range(1, N2 - 1), pad2, 1)
    for s in (0, N2 + 1):
        pad2[s] = jnp.zeros((N2 + 2, Z, L), F32)
        pad2[:, s : s + 1] = jnp.zeros((N2 + 2, 1, Z, L), F32)
    for c in loads[1:]:
        c.wait()
    wf[...] = jnp.zeros(wf.shape, BF)
    for j in range(3):
        for k in range(3):
            t = (j * 3 + k) * L
            wf[t : t + C2, 0:C2] = wf_ref[j, k]
    fine_columns()

    def fine_forward(chunk, _):
        act = rounded(elu(nn(fine_rows(chunk), wf[...])))
        fa[pl.ds(chunk * 4, 4)] = act.reshape(4, N2, Z, L)
        return 0

    lax.fori_loop(0, 4, fine_forward, 0)

    take_halo(EX_IN, pad2, N2, 1, copies)
    inner = N2 - 2
    for j in range(3):
        for k in range(3):
            t = (j * 3 + k) * L
            at = 0
            for ys, xs in (
                (slice(j, j + 1), slice(k, k + N2)),
                (slice(N2 - 1 + j, N2 + j), slice(k, k + N2)),
                (slice(1 + j, 1 + j + inner), slice(k, k + 1)),
                (slice(1 + j, 1 + j + inner), slice(N2 - 1 + k, N2 + k)),
            ):
                part = pad2[ys, xs].reshape(-1, L).astype(BF)
                q[at : at + part.shape[0], t : t + L] = part
                at += part.shape[0]
    rim = rounded(elu(nn(q[0:at, :], wf[...]))).reshape(-1, Z, L)
    fa[0] = rim[0:N2]
    fa[N2 - 1] = rim[N2 : 2 * N2]
    fa[1 : N2 - 1, 0:1] = rim[2 * N2 : 2 * N2 + inner].reshape(inner, 1, Z, L)
    fa[1 : N2 - 1, N2 - 1 : N2] = rim[2 * N2 + inner :].reshape(inner, 1, Z, L)
    v = fa[...].reshape(N3, 2, N3, 2, Z, L)
    v = (v[:, 0, :, 0] + v[:, 0, :, 1]) + (v[:, 1, :, 0] + v[:, 1, :, 1])
    pad3[3 : N3 + 3, 3 : N3 + 3] = rounded(0.25 * v)
    copies = send_halo(EX_POOL, pad3, N3, 3)

    spread(u_ref)
    read_rows(0, N2, range(N2), e32, 0)
    low = e32[...].reshape(N3, 2, N3, 2, Z, L)
    low = (low[:, 0, :, 0] + low[:, 0, :, 1]) + (low[:, 1, :, 0] + low[:, 1, :, 1])
    ulp[1 : N3 + 1, 1 : N3 + 1] = rounded(low)
    low_copies = send_halo(EX_LOW, ulp, N3, 1)
    for ref in (wft, we, wet, wm, wmt, wl):
        ref[...] = jnp.zeros(ref.shape, BF)
    wl[0:C2, 0:C3] = wl_ref[...]
    for j in range(3):
        for k in range(3):
            t = (j * 3 + k) * L
            wft[0:C2, t : t + C2] = wf_ref[2 - j, 2 - k]
            for i in range(3):
                we[t : t + C2, i * L : i * L + C3] = we_ref[i, j, k]
                wm[t : t + C3, i * L : i * L + C3] = wm_ref[i, j, k]
                wet[i * L : i * L + C2, t : t + C3] = we_ref[2 - i, 2 - j, 2 - k]
                wmt[i * L : i * L + C3, t : t + C3] = wm_ref[2 - i, 2 - j, 2 - k]
    fine_columns()

    take_halo(EX_POOL, pad3, N3, 3, copies)
    c1p[...] = rounded(elu(joined(nn(columns(pad3, N3 + 4), we[...])))).reshape(N3 + 4, N3 + 4, Z, L)
    for there, ys, xs in (
        (gy > 0, slice(0, 2), slice(None)),
        (gy < GY - 1, slice(N3 + 2, N3 + 4), slice(None)),
        (gx > 0, slice(None), slice(0, 2)),
        (gx < GX - 1, slice(None), slice(N3 + 2, N3 + 4)),
    ):
        c1p[ys, xs] = c1p[ys, xs] * jnp.where(there, 1.0, 0.0).astype(F32)
    two = rounded(elu(joined(nn(columns(c1p, N3 + 2), wm[...]))))
    c2[...] = two.reshape(N3 + 2, N3 + 2, Z, L)
    take_halo(EX_LOW, ulp, N3, 1, low_copies)
    back = nn(ulp[...].reshape(-1, L).astype(BF), wl[...]).reshape(-1, Z, L)
    gp[...] = rounded(back * slope(two)).reshape(N3 + 2, N3 + 2, Z, L)
    own = c1p[2 : N3 + 2, 2 : N3 + 2].reshape(-1, Z, L)
    g1 = rounded(joined(nt(columns(gp, N3), wmt[...])) * slope(own))
    gup[1 : N3 + 1, 1 : N3 + 1] = g1.reshape(N3, N3, Z, L)
    copies = send_halo(EX_G1, gup, N3, 1)

    mid = coarse_weight_grad(
        columns(c1p, N3, 1), gp[1 : N3 + 1, 1 : N3 + 1].reshape(-1, Z, L)
    )
    two = c2[1 : N3 + 1, 1 : N3 + 1].reshape(-1, L).astype(BF)
    lift_grad = tn(ulp[1 : N3 + 1, 1 : N3 + 1].reshape(-1, L).astype(BF), two)
    blocks = [mid[t, :C3, i * L : (i + 1) * L] for i in range(3) for t in range(9)]
    blocks.append(lift_grad[:C3])
    for g in range(7):
        for d, part in enumerate(pack4(blocks[4 * g : 4 * g + 4])):
            m0[(g * 3 + d) * C3 : (g * 3 + d + 1) * C3, :] = part.astype(BF)
    m0[21 * C3 :, :] = jnp.zeros((ROWS_M - 21 * C3, L), BF)
    red_m = Reduce(ring, ROWS_M, (m0, m1), (mr0, mr1), mslot, mout, m_send, m_recv, sent)
    red_m.scatter_start(0)
    ent = coarse_weight_grad(columns(pad3, N3, 2), gup[1 : N3 + 1, 1 : N3 + 1].reshape(-1, Z, L))
    blocks = [ent[t, :C2, i * L : (i + 1) * L] for i in range(3) for t in range(9)]
    blocks.append(jnp.zeros((C2, L), F32))
    for g in range(7):
        for d, part in enumerate(pack4(blocks[4 * g : 4 * g + 4])):
            are32[(g * 3 + d) * C2 : (g * 3 + d + 1) * C2, :] = part
    are32[21 * C2 :, :] = jnp.zeros((ROWS_E - 21 * C2, L), F32)
    e0[...] = are32[...].astype(BF)
    red_e = Reduce(ring, ROWS_E, (e0, e1), (er0, er1), eslot, eout, e_send, e_recv, sent)
    red_e.scatter_start(0)
    red_m.scatter_end(0)
    red_m.scatter_start(1)

    take_halo(EX_G1, gup, N3, 1, copies)
    low = rounded(joined(nt(columns(gup, N3), wet[...])))
    gup[0:N3, 0:N3] = 0.25 * low.reshape(N3, N3, Z, L)
    red_e.scatter_end(0)
    red_e.scatter_start(1)

    for j in range(3):
        for y in range(N2 + 2):
            if not 0 <= y - j < N2:
                g3f[y, :, j * L : (j + 1) * L] = jnp.zeros((N2 * Z, L), BF)

    def fine_back(y, _):
        act = fa[pl.ds(y * 2, 2)].reshape(2, N3, 2, Z, L)
        e = e32[pl.ds(y * 2, 2)].reshape(2, N3, 2, Z, L)
        up = gup[pl.ds(y, 1), 0:N3].reshape(1, N3, 1, Z, L)
        g = ((e + up) * slope(act)).reshape(2, N2 * Z, L).astype(BF)
        for j in range(3):
            g3f[pl.ds(y * 2 + j, 2), :, j * L : (j + 1) * L] = g
        pad2[pl.ds(y * 2 + 1, 2), 1 : N2 + 1] = g.astype(F32).reshape(2, N2, Z, L)
        return 0

    lax.fori_loop(0, N3, fine_back, 0)
    copies = send_halo(EX_FINE, pad2, N2, 1)

    grad = tn(x3[...].reshape(-1, 3 * L), g3f[...].reshape(-1, 3 * L))
    for k in range(3):
        b0, b1, b2 = [grad[k * L : k * L + C2, j * L : (j + 1) * L] for j in range(3)]
        lane = lanes(b0.shape)
        r1, r2 = pltpu.roll(b1, C2, 1), pltpu.roll(b2, 2 * C2 - L, 1)
        arf32[2 * k * C2 : (2 * k + 1) * C2, :] = jnp.where(lane < C2, b0, r1)
        arf32[(2 * k + 1) * C2 : (2 * k + 2) * C2, :] = jnp.where(lane < 2 * C2 - L, r1, r2)
    arf32[6 * C2 :, :] = jnp.zeros((ROWS_F - 6 * C2, L), F32)
    f0[...] = arf32[...].astype(BF)
    red_f = Reduce(ring, ROWS_F, (f0, f1), (fr0, fr1), fslot, fout, f_send, f_recv, sent)
    red_f.scatter_start(0)
    red_m.scatter_end(1)
    red_m.last_start()
    red_f.scatter_end(0)
    red_f.scatter_start(1)

    two = c2[1 : N3 + 1, 1 : N3 + 1].reshape(-1, L).astype(BF)
    gup[0:N3, 0:N3] = rounded(nt(two, wl[...])).reshape(N3, N3, Z, L)

    def mix(y, _):
        act = fa[pl.ds(y * 2, 2)].reshape(2, N3, 2, Z, L)
        up = gup[pl.ds(y, 1), 0:N3].reshape(1, N3, 1, Z, L)
        d32[pl.ds(y * 2, 2)] = (act + up).reshape(2, N2, Z, L)
        return 0

    lax.fori_loop(0, N3, mix, 0)

    red_e.scatter_end(1)
    red_e.last_start()
    red_m.last_end()
    red_m.gather_start(1)

    write_cells(d32, raw, mixed_ref)
    stores = [pltpu.make_async_copy(mixed_ref, mixed_hbm, out_sem.at[0])]
    stores[0].start()

    red_f.scatter_end(1)
    red_f.last_start()
    red_e.last_end()
    red_e.gather_start(1)

    take_halo(EX_FINE, pad2, N2, 1, copies)
    fine_columns()

    def fine_backward(chunk, _):
        d32[pl.ds(chunk * 4, 4)] = nt(fine_rows(chunk), wft[...]).reshape(4, N2, Z, L)
        return 0

    lax.fori_loop(0, 4, fine_backward, 0)

    red_f.last_end()
    red_f.gather_start(1)

    write_cells(d32, raw2, ig_ref)
    stores.append(pltpu.make_async_copy(ig_ref, ig_hbm, out_sem.at[1]))
    stores[1].start()

    red_m.gather_end()
    red_m.gather_start(0)
    red_e.gather_end()
    red_e.gather_start(0)
    red_f.gather_end()
    red_f.gather_start(0)
    for c in stores:
        c.wait()
    red_m.gather_end()
    red_e.gather_end()
    red_f.gather_end()
    for c in sent:
        c.wait_send()


def finish(mixed_in, ig_in, mout, eout, fout, mixed, ig, gf_ref, ge_ref, gm_ref, gl_ref, are32, arf32, sem):
    copies = [
        pltpu.make_async_copy(mixed_in, mixed, sem.at[0]),
        pltpu.make_async_copy(ig_in, ig, sem.at[1]),
    ]
    for c in copies:
        c.start()
    for g in range(7):
        d = [mout[(g * 3 + s) * C3 : (g * 3 + s + 1) * C3, :].astype(F32) for s in range(3)]
        for s, b in enumerate(unpack4(d)):
            t = g * 4 + s
            if t < 27:
                gm_ref[t // 9, (t // 3) % 3, t % 3] = b[:, 0:C3]
            else:
                gl_ref[...] = b[0:C2, 0:C3]
    are32[...] = eout[...].astype(F32)
    for g in range(7):
        d = [are32[(g * 3 + s) * C2 : (g * 3 + s + 1) * C2, :] for s in range(3)]
        for s, b in enumerate(unpack4(d)):
            t = g * 4 + s
            if t < 27:
                ge_ref[t // 9, (t // 3) % 3, t % 3] = b[:, 0:C3]
    arf32[...] = fout[...].astype(F32)
    for k in range(3):
        d0 = arf32[2 * k * C2 : (2 * k + 1) * C2, :]
        d1 = arf32[(2 * k + 1) * C2 : (2 * k + 2) * C2, :]
        lane = lanes(d0.shape)
        b1 = pltpu.roll(jnp.where(lane >= C2, d0, d1), L - C2, 1)
        b2 = pltpu.roll(d1, 2 * L - 2 * C2, 1)
        for j, b in enumerate((d0, b1, b2)):
            gf_ref[j, k] = b[:, 0:C2]
    for c in copies:
        c.wait()


def body(fine_input, fine_weight, entry_weight, middle_weight, lift_weight, upstream):
    args = (fine_input, fine_weight, entry_weight, middle_weight, lift_weight.T, upstream)
    field = jax.ShapeDtypeStruct(fine_input.shape, BF)
    vmem = pl.BlockSpec(memory_space=pltpu.VMEM)
    whole = pl.BlockSpec(memory_space=pl.ANY)
    cells3 = (N3 + 4) * (N3 + 4) * Z

    def v(*shape):
        return pltpu.VMEM(shape, BF)

    def w(*shape):
        return pltpu.VMEM(shape, F32)

    def sems(n):
        return [pltpu.SemaphoreType.DMA((n,)), pltpu.SemaphoreType.DMA((n,))]

    def sums(rows):
        return [
            v(rows, L), v(rows // 2, L),
            v(1, rows // 2, L), v(15, rows // 32, L), v(4, rows // 32, L),
            *sems(35),
        ]

    scratch = [
        *[v(*arg.shape) for arg in args], v(*field.shape), v(*field.shape), *sems(6),
        w(TILES, Z * N2, L), w(TILES, Z * N2, L), w(N2 + 2, N2 + 2, Z, L), w(N3 + 6, N3 + 6, Z, L),
        w(N3 + 2, N3 + 2, Z, L), w(N2, N2, Z, L),
        v(N2 + 2, N2 * Z, 3 * L), v(N2 + 2, N2 * Z, 3 * L), w(N2, N2, Z, L),
        v(cells3, 9 * L), w(N3 + 4, N3 + 4, Z, L), w(N3 + 2, N3 + 2, Z, L), w(N3 + 2, N3 + 2, Z, L),
        w(N3 + 2, N3 + 2, Z, L), w(N2, N2, Z, L),
        v(9 * L, L), v(L, 9 * L), v(9 * L, 3 * L), v(3 * L, 9 * L), v(9 * L, 3 * L), v(3 * L, 9 * L), v(L, L),
        w(ROWS_E, L), w(ROWS_F, L),
        v(5, 8, 3 * N3 * Z, L), v(5, 8, 3 * N3 * Z, L), *sems(40),
        *sums(ROWS_M), *sums(ROWS_E), *sums(ROWS_F),
    ]
    packed = [jax.ShapeDtypeStruct((rows, L), BF) for rows in (ROWS_M, ROWS_E, ROWS_F)]
    fields_and_sums = pl.pallas_call(
        kernel,
        out_shape=(field, field, *packed),
        in_specs=[whole] * 6,
        out_specs=[whole] * 2 + [vmem] * 3,
        scratch_shapes=scratch,
        compiler_params=pltpu.CompilerParams(
            collective_id=0, has_side_effects=True, vmem_limit_bytes=60 * 1024 * 1024
        ),
    )(*args)
    mixed, input_grad, fine, entry, middle, lift = pl.pallas_call(
        finish,
        out_shape=(
            field,
            field,
            jax.ShapeDtypeStruct(fine_weight.shape, F32),
            jax.ShapeDtypeStruct(entry_weight.shape, F32),
            jax.ShapeDtypeStruct(middle_weight.shape, F32),
            jax.ShapeDtypeStruct(lift_weight.shape[::-1], F32),
        ),
        in_specs=[whole] * 2 + [vmem] * 3,
        out_specs=[whole] * 2 + [vmem] * 4,
        scratch_shapes=[w(ROWS_E, L), w(ROWS_F, L), pltpu.SemaphoreType.DMA((2,))],
        compiler_params=pltpu.CompilerParams(vmem_limit_bytes=32 * 1024 * 1024),
    )(*fields_and_sums)
    return mixed, input_grad, fine, entry, middle, lift.T


def solution(mesh):
    assert mesh.shape["gy"] == GY and mesh.shape["gx"] == GX
    return jax.shard_map(
        body,
        mesh=mesh,
        in_specs=(P("dp", None, "gy", "gx"), P(), P(), P(), P(), P("dp", None, "gy", "gx")),
        out_specs=(P("dp", None, "gy", "gx"), P("dp", None, "gy", "gx"), P(), P(), P(), P()),
        check_vma=False,
    )
```

time: 85.4 us -> 61.1 us (0.72)
  Pallas kernels: 74.2 us -> 55.3 us
  local copies, waits for them, and re-layouts: 10.2 us -> 4.86 us
    pallas_call x1 -> x2, Pallas kernels: 74.2 us -> 55.3 us  [the longest x1 52.8 us: body(): pl.pallas_call(kernel, out_shape=(field, field, *packed), in_specs=[whole...]
    unnamed x10, local copies, waits for them, and re-layouts: 8.66 us -> 4.86 us
    pallas_call x1 -> x0, local copies, waits for them, and re-layouts: 1.58 us -> none  [body(): pl.pallas_call(kernel, out_shape=(field, field, jax.ShapeDtypeStruct(fine...]
where the time goes in v2:
time: 61.1 us; the launch traced here: 60.8 us
  Pallas kernels  55.3 us (91%)
  local copies, waits for them, and re-layouts  4.86 us (8%)
  between operations  0.65 us (1%)
    pallas_call x1, Pallas kernels, body(): pl.pallas_call(kernel, out_shape=(field, field, *packed), in_specs=[whole...  52.8 us
    unnamed x10, local copies, waits for them, and re-layouts  4.86 us
    pallas_call x1, Pallas kernels, body(): pl.pallas_call(finish, out_shape=(field, field, jax.ShapeDtypeStruct(fine...  2.45 us

profile of v2, /device:TPU:1, one launch (start us, length us, event | category | flops | bytes accessed | tf_op | source)
XLA Modules:
  0.0 60.8 jit_solution(227825200525762381)
XLA Ops:
  0.6 52.8 %shard_map.109 = (bf16[1,8,16,1152]{3,2,1,0:T(8,128)(2,1)}, bf16[1,8,16,1152]{3,2,1,0:T(8,128)(2,1)}, bf16[2048,128]{1,0:T(8,128)(2,1)}, bf16[1536,128]{1,0:T(8,128)(2,1)}, bf16[512,128]{1,0:T(8,128)(2,1)}) custom-call(bf16[1,8,16,1152]{3,2,1,0:T(8,128)(2,1)} %a_hbm.1, bf16[3,3,72,72]{3,2,1,0:T(8,128)(2,1)} %wf_hbm.1, bf16[3,3,3,72,96]{4,3,2,1,0:T(8,128)(2,1)} %we_hbm.1, ...), custom_call_target="tpu_custom_call" | custom-call | tf_op jit(solution)/shard_map/pallas_call | solution.py:635
  53.5 0.0 copy-start
  53.5 1.0 %copy-done = bf16[2048,128]{1,0:T(8,128)(2,1)S(1)} copy-done((bf16[2048,128]{1,0:T(8,128)(2,1)S(1)}, bf16[2048,128]{1,0:T(8,128)(2,1)}, u32[]{:S(2)}) %copy-start) | copy-done | bytes 524312
  54.5 0.0 copy-start.1
  54.5 1.0 %copy-done.1 = bf16[1536,128]{1,0:T(8,128)(2,1)S(1)} copy-done((bf16[1536,128]{1,0:T(8,128)(2,1)S(1)}, bf16[1536,128]{1,0:T(8,128)(2,1)}, u32[]{:S(2)}) %copy-start.1) | copy-done | bytes 393240
  55.5 0.0 copy-start.2
  55.5 1.0 %copy-done.2 = bf16[1,8,16,1152]{3,2,1,0:T(8,128)(2,1)S(1)} copy-done((bf16[1,8,16,1152]{3,2,1,0:T(8,128)(2,1)S(1)}, bf16[1,8,16,1152]{3,2,1,0:T(8,128)(2,1)}, u32[]{:S(2)}) %copy-start.2) | copy-done | bytes 294936
  56.5 0.0 copy-start.3
  56.5 1.0 %copy-done.3 = bf16[1,8,16,1152]{3,2,1,0:T(8,128)(2,1)S(1)} copy-done((bf16[1,8,16,1152]{3,2,1,0:T(8,128)(2,1)S(1)}, bf16[1,8,16,1152]{3,2,1,0:T(8,128)(2,1)}, u32[]{:S(2)}) %copy-start.3) | copy-done | bytes 294936
  57.4 0.0 copy-start.4
  57.4 0.9 %copy-done.4 = bf16[512,128]{1,0:T(8,128)(2,1)S(1)} copy-done((bf16[512,128]{1,0:T(8,128)(2,1)S(1)}, bf16[512,128]{1,0:T(8,128)(2,1)}, u32[]{:S(2)}) %copy-start.4) | copy-done | bytes 131096
  58.3 2.5 %shard_map.110 = (bf16[1,8,16,1152]{3,2,1,0:T(8,128)(2,1)}, bf16[1,8,16,1152]{3,2,1,0:T(8,128)(2,1)}, f32[3,3,72,72]{3,2,1,0:T(8,128)}, f32[3,3,3,72,96]{4,3,2,1...) custom-call(bf16[1,8,16,1152]{3,2,1,0:T(8,128)(2,1)S(1)} %copy-done.2, ...), custom_call_target="tpu_custom_call" | custom-call | tf_op jit(solution)/shard_map/pallas_call | solution.py:645
Async XLA Ops:
  53.5 1.0 %copy-start = (bf16[2048,128]{1,0:T(8,128)(2,1)S(1)}, bf16[2048,128]{1,0:T(8,128)(2,1)}, u32[]{:S(2)}) copy-start(bf16[2048,128]{1,0:T(8,128)(2,1)} %get-tuple-element.19.mout) | copy-start | bytes 1572868
  54.5 1.0 %copy-start.1 = (bf16[1536,128]{1,0:T(8,128)(2,1)S(1)}, bf16[1536,128]{1,0:T(8,128)(2,1)}, u32[]{:S(2)}) copy-start(bf16[1536,128]{1,0:T(8,128)(2,1)} %get-tuple-element.20.eout) | copy-start | bytes 1179652
  55.5 1.0 %copy-start.2 = (bf16[1,8,16,1152]{3,2,1,0:T(8,128)(2,1)S(1)}, bf16[1,8,16,1152]{3,2,1,0:T(8,128)(2,1)}, u32[]{:S(2)}) copy-start(bf16[1,8,16,1152]{3,2,1,0:T(8,128)(2,1)} %get-tuple-element.17.mixed_in) | copy-start | bytes 884740
  56.5 1.0 %copy-start.3 = (bf16[1,8,16,1152]{3,2,1,0:T(8,128)(2,1)S(1)}, bf16[1,8,16,1152]{3,2,1,0:T(8,128)(2,1)}, u32[]{:S(2)}) copy-start(bf16[1,8,16,1152]{3,2,1,0:T(8,128)(2,1)} %get-tuple-element.18.ig_in) | copy-start | bytes 884740
  57.4 0.9 %copy-start.4 = (bf16[512,128]{1,0:T(8,128)(2,1)S(1)}, bf16[512,128]{1,0:T(8,128)(2,1)}, u32[]{:S(2)}) copy-start(bf16[512,128]{1,0:T(8,128)(2,1)} %get-tuple-element.21.fout) | copy-start | bytes 393220

commit v3 on v2

--- a/solution.py
+++ b/solution.py
@@ -19,13 +19,15 @@
 GX = 8
 MERGED = N2 * C2
 TILES = MERGED // L
-DIRS = [(dy, dx) for dy in (-1, 0, 1) for dx in (-1, 0, 1) if (dy, dx) != (0, 0)]
+DIRS = [(-1, 0), (1, 0), (-1, -1), (-1, 1), (1, -1), (1, 1), (0, -1), (0, 1)]
 
 EX_IN, EX_POOL, EX_LOW, EX_G1, EX_FINE = range(5)
 
 ROWS_M = 2048
 ROWS_E = 1536
 ROWS_F = 512
+ROWS = (ROWS_M, ROWS_E, ROWS_F)
+PITCH = 80
 
 
 def lanes(shape):
@@ -71,6 +73,10 @@
     def member(self, kind):
         if kind == "dp":
             return self.dp
+        if kind == "y":
+            return self.gx // 2
+        if kind == "x":
+            return self.gy // 2
         if kind == "xy":
             return (self.gy // 2) * 4 + self.gx // 2
         return (self.gy % 2) * 2 + self.gx % 2
@@ -78,6 +84,10 @@
     def device(self, kind, p):
         if kind == "dp":
             return (p, self.gy, self.gx)
+        if kind == "y":
+            return (self.dp, self.gy, p * 2 + self.gx % 2)
+        if kind == "x":
+            return (self.dp, p * 2 + self.gy % 2, self.gx)
         if kind == "xy":
             return (self.dp, (p // 4) * 2 + self.gy % 2, (p % 4) * 2 + self.gx % 2)
         return (self.dp, (self.gy // 2) * 2 + p // 2, (self.gx // 2) * 2 + p % 2)
@@ -86,22 +96,22 @@
         m = self.member(kind)
         if kind == "dp":
             return [1 - m]
-        if kind == "z":
+        if kind in ("x", "y", "z"):
             return [(m + r) % 4 for r in (2, 1, 3)]
         steps = [(2, 2), (2, 1), (1, 2), (2, 3), (3, 2), (1, 1), (1, 3), (3, 1), (3, 3)]
         steps += [(2, 0), (0, 2), (1, 0), (0, 1), (3, 0), (0, 3)]
         return [((m // 4 + x) % 4) * 4 + (m % 4 + y) % 4 for x, y in steps]
 
 
-SIZE = {"dp": 2, "xy": 16, "z": 4}
+SIZE = {"dp": 2, "x": 4, "y": 4, "xy": 16, "z": 4}
 
 
 class Reduce:
-    scatter = ("dp", "xy")
     last = "z"
 
-    def __init__(self, ring, rows, bufs, recvs, slots, out, send, recv, sent):
+    def __init__(self, ring, rows, scatter, bufs, recvs, slots, out, send, recv, sent):
         self.ring = ring
+        self.scatter = scatter
         self.bufs = bufs
         self.recvs = recvs
         self.slots = slots
@@ -201,9 +211,9 @@
 
 def kernel(
     a_hbm, wf_hbm, we_hbm, wm_hbm, wl_hbm, u_hbm,
-    mixed_hbm, ig_hbm, mout, eout, fout,
-    a_ref, wf_ref, we_ref, wm_ref, wl_ref, u_ref, mixed_ref, ig_ref, in_sem, out_sem,
-    raw, raw2, pad2, pad3, ulp, e32, x3, g3f, fa, q, c1p, c2, gp, gup, d32,
+    mixed_hbm, ig_hbm, m_hbm, e_hbm, f_hbm,
+    a_ref, wf_ref, we_ref, wm_ref, wl_ref, u_ref, mixed_ref, ig_ref, mout, eout, fout, mflat, eflat, in_sem, out_sem,
+    raw, raw2, pad2, pad3, ulp, e32, x3, g3f, fa, q, c1p, c2, gp, gup, up, gsum, grim, d32,
     wf, wft, we, wet, wm, wmt, wl, are32, arf32,
     sbuf, rbuf, h_send, h_recv,
     m0, m1, mr0, mr1, mslot, m_send, m_recv,
@@ -212,12 +222,6 @@
 ):
     ring = Ring()
     dp, gy, gx = ring.dp, ring.gy, ring.gx
-
-    barrier = pltpu.get_barrier_semaphore()
-    met = [(dp, (gy + dy + GY) % GY, (gx + dx + GX) % GX) for dy, dx in DIRS]
-    met += [ring.device(kind, p) for kind in ("dp", "xy") for p in ring.others(kind)]
-    for device in met:
-        pl.semaphore_signal(barrier, inc=1, device_id=device, device_id_type=MESH)
 
     loads = [
         pltpu.make_async_copy(src, dst, in_sem.at[i])
@@ -228,10 +232,21 @@
             )
         )
     ]
-    for c in loads:
-        c.start()
+    for load in loads:
+        load.start()
+
+    barrier = pltpu.get_barrier_semaphore()
+    met = [(dp, (gy + dy + GY) % GY, (gx + dx + GX) % GX) for dy, dx in DIRS]
+    met += [ring.device(kind, p) for kind in ("dp", "xy") for p in ring.others(kind)]
+    for device in met:
+        pl.semaphore_signal(barrier, inc=1, device_id=device, device_id_type=MESH)
 
     sent = []
+    stores = []
+
+    def store(src, dst):
+        stores.append(pltpu.make_async_copy(src, dst, out_sem.at[len(stores)]))
+        stores[-1].start()
 
     def edge(step, n, w):
         return {1: slice(n, n + w), -1: slice(w, 2 * w), 0: slice(w, n + w)}[step]
@@ -338,6 +353,27 @@
                 )
         return q[0:rows, :]
 
+    def tap_rows(ref, blocks, at=0):
+        for y0, y1, x0, x1 in blocks:
+            rows = (y1 - y0) * (x1 - x0) * Z
+            for j in range(3):
+                for k in range(3):
+                    t = (j * 3 + k) * L
+                    part = ref[y0 + j : y1 + j, x0 + k : x1 + k]
+                    q[at : at + rows, t : t + L] = part.reshape(rows, L).astype(BF)
+            at += rows
+        return q[0:at, :]
+
+    def put_rows(dst, blocks, cells):
+        at = 0
+        for y0, y1, x0, x1 in blocks:
+            n = (y1 - y0) * (x1 - x0)
+            dst[y0:y1, x0:x1] = cells[at : at + n].reshape(y1 - y0, x1 - x0, Z, L)
+            at += n
+
+    def rim(n, w):
+        return [(0, w, 0, n), (n - w, n, 0, n), (w, n - w, 0, w), (w, n - w, n - w, n)]
+
     def joined(acc):
         acc = acc.reshape(-1, Z, 3 * L)
         return shift_z(acc[:, :, 0:L], 1) + acc[:, :, L : 2 * L] + shift_z(acc[:, :, 2 * L :], -1)
@@ -359,8 +395,8 @@
     for s in (0, N2 + 1):
         pad2[s] = jnp.zeros((N2 + 2, Z, L), F32)
         pad2[:, s : s + 1] = jnp.zeros((N2 + 2, 1, Z, L), F32)
-    for c in loads[1:]:
-        c.wait()
+    for load in loads[1:]:
+        load.wait()
     wf[...] = jnp.zeros(wf.shape, BF)
     for j in range(3):
         for k in range(3):
@@ -376,25 +412,7 @@
     lax.fori_loop(0, 4, fine_forward, 0)
 
     take_halo(EX_IN, pad2, N2, 1, copies)
-    inner = N2 - 2
-    for j in range(3):
-        for k in range(3):
-            t = (j * 3 + k) * L
-            at = 0
-            for ys, xs in (
-                (slice(j, j + 1), slice(k, k + N2)),
-                (slice(N2 - 1 + j, N2 + j), slice(k, k + N2)),
-                (slice(1 + j, 1 + j + inner), slice(k, k + 1)),
-                (slice(1 + j, 1 + j + inner), slice(N2 - 1 + k, N2 + k)),
-            ):
-                part = pad2[ys, xs].reshape(-1, L).astype(BF)
-                q[at : at + part.shape[0], t : t + L] = part
-                at += part.shape[0]
-    rim = rounded(elu(nn(q[0:at, :], wf[...]))).reshape(-1, Z, L)
-    fa[0] = rim[0:N2]
-    fa[N2 - 1] = rim[N2 : 2 * N2]
-    fa[1 : N2 - 1, 0:1] = rim[2 * N2 : 2 * N2 + inner].reshape(inner, 1, Z, L)
-    fa[1 : N2 - 1, N2 - 1 : N2] = rim[2 * N2 + inner :].reshape(inner, 1, Z, L)
+    put_rows(fa, rim(N2, 1), rounded(elu(nn(tap_rows(pad2, rim(N2, 1)), wf[...]))).reshape(-1, Z, L))
     v = fa[...].reshape(N3, 2, N3, 2, Z, L)
     v = (v[:, 0, :, 0] + v[:, 0, :, 1]) + (v[:, 1, :, 0] + v[:, 1, :, 1])
     pad3[3 : N3 + 3, 3 : N3 + 3] = rounded(0.25 * v)
@@ -419,9 +437,13 @@
                 wet[i * L : i * L + C2, t : t + C3] = we_ref[2 - i, 2 - j, 2 - k]
                 wmt[i * L : i * L + C3, t : t + C3] = wm_ref[2 - i, 2 - j, 2 - k]
     fine_columns()
+    g3f[...] = jnp.zeros(g3f.shape, BF)
+    inner = [(3, N3 + 1, 3, N3 + 1)]
+    put_rows(c1p, inner, rounded(elu(joined(nn(tap_rows(pad3, inner), we[...])))))
 
     take_halo(EX_POOL, pad3, N3, 3, copies)
-    c1p[...] = rounded(elu(joined(nn(columns(pad3, N3 + 4), we[...])))).reshape(N3 + 4, N3 + 4, Z, L)
+    outer = rim(N3 + 4, 3)
+    put_rows(c1p, outer, rounded(elu(joined(nn(tap_rows(pad3, outer), we[...])))))
     for there, ys, xs in (
         (gy > 0, slice(0, 2), slice(None)),
         (gy < GY - 1, slice(N3 + 2, N3 + 4), slice(None)),
@@ -450,7 +472,7 @@
         for d, part in enumerate(pack4(blocks[4 * g : 4 * g + 4])):
             m0[(g * 3 + d) * C3 : (g * 3 + d + 1) * C3, :] = part.astype(BF)
     m0[21 * C3 :, :] = jnp.zeros((ROWS_M - 21 * C3, L), BF)
-    red_m = Reduce(ring, ROWS_M, (m0, m1), (mr0, mr1), mslot, mout, m_send, m_recv, sent)
+    red_m = Reduce(ring, ROWS_M, ("dp", "xy"), (m0, m1), (mr0, mr1), mslot, mout, m_send, m_recv, sent)
     red_m.scatter_start(0)
     ent = coarse_weight_grad(columns(pad3, N3, 2), gup[1 : N3 + 1, 1 : N3 + 1].reshape(-1, Z, L))
     blocks = [ent[t, :C2, i * L : (i + 1) * L] for i in range(3) for t in range(9)]
@@ -460,45 +482,65 @@
             are32[(g * 3 + d) * C2 : (g * 3 + d + 1) * C2, :] = part
     are32[21 * C2 :, :] = jnp.zeros((ROWS_E - 21 * C2, L), F32)
     e0[...] = are32[...].astype(BF)
-    red_e = Reduce(ring, ROWS_E, (e0, e1), (er0, er1), eslot, eout, e_send, e_recv, sent)
+    red_e = Reduce(ring, ROWS_E, ("dp", "xy"), (e0, e1), (er0, er1), eslot, eout, e_send, e_recv, sent)
     red_e.scatter_start(0)
     red_m.scatter_end(0)
     red_m.scatter_start(1)
 
-    take_halo(EX_G1, gup, N3, 1, copies)
-    low = rounded(joined(nt(columns(gup, N3), wet[...])))
-    gup[0:N3, 0:N3] = 0.25 * low.reshape(N3, N3, Z, L)
+    inner = [(1, N3 - 1, 1, N3 - 1)]
+    low = rounded(joined(nt(tap_rows(gup, inner), wet[...])))
+    put_rows(up, inner, 0.25 * low)
+
+    def fine_back(y, _):
+        act = fa[pl.ds(y * 2, 2), 2 : N2 - 2].reshape(2, N3 - 2, 2, Z, L)
+        e = e32[pl.ds(y * 2, 2), 2 : N2 - 2].reshape(2, N3 - 2, 2, Z, L)
+        g = e + up[pl.ds(y, 1), 1 : N3 - 1].reshape(1, N3 - 2, 1, Z, L)
+        g = (g * slope(act)).reshape(2, (N2 - 4) * Z, L).astype(BF)
+        for j in range(3):
+            g3f[pl.ds(y * 2 + j, 2), 2 * Z : (N2 - 2) * Z, j * L : (j + 1) * L] = g
+        pad2[pl.ds(y * 2 + 1, 2), 3 : N2 - 1] = g.astype(F32).reshape(2, N2 - 4, Z, L)
+        return 0
+
+    lax.fori_loop(1, N3 - 1, fine_back, 0)
     red_e.scatter_end(0)
     red_e.scatter_start(1)
-
-    for j in range(3):
-        for y in range(N2 + 2):
-            if not 0 <= y - j < N2:
-                g3f[y, :, j * L : (j + 1) * L] = jnp.zeros((N2 * Z, L), BF)
-
-    def fine_back(y, _):
-        act = fa[pl.ds(y * 2, 2)].reshape(2, N3, 2, Z, L)
-        e = e32[pl.ds(y * 2, 2)].reshape(2, N3, 2, Z, L)
-        up = gup[pl.ds(y, 1), 0:N3].reshape(1, N3, 1, Z, L)
-        g = ((e + up) * slope(act)).reshape(2, N2 * Z, L).astype(BF)
+    gsum[...] = tn(x3[...].reshape(-1, 3 * L), g3f[...].reshape(-1, 3 * L))
+    start = at = 4 * (N3 - 1) * Z
+    for y0, y1, x0, x1 in rim(N2, 2):
+        rows = (y1 - y0) * (x1 - x0) * Z
         for j in range(3):
-            g3f[pl.ds(y * 2 + j, 2), :, j * L : (j + 1) * L] = g
-        pad2[pl.ds(y * 2 + 1, 2), 1 : N2 + 1] = g.astype(F32).reshape(2, N2, Z, L)
-        return 0
-
-    lax.fori_loop(0, N3, fine_back, 0)
+            part = x3[y0 + j : y1 + j, x0 * Z : x1 * Z, :].reshape(rows, 3 * L)
+            q[at : at + rows, 3 * j * L : 3 * (j + 1) * L] = part
+        at += rows
+
+    take_halo(EX_G1, gup, N3, 1, copies)
+    low = rounded(joined(nt(tap_rows(gup, rim(N3, 1)), wet[...])))
+    put_rows(up, rim(N3, 1), 0.25 * low)
+    rows = 0
+    for y0, y1, x0, x1 in rim(N2, 2):
+        ny, nx = (y1 - y0) // 2, (x1 - x0) // 2
+        act = fa[y0:y1, x0:x1].reshape(ny, 2, nx, 2, Z, L)
+        e = e32[y0:y1, x0:x1].reshape(ny, 2, nx, 2, Z, L)
+        g = e + up[y0 // 2 : y1 // 2, x0 // 2 : x1 // 2].reshape(ny, 1, nx, 1, Z, L)
+        g = (g * slope(act)).reshape(-1, L).astype(BF)
+        grim[rows : rows + g.shape[0], :] = g
+        rows += g.shape[0]
+        pad2[y0 + 1 : y1 + 1, x0 + 1 : x1 + 1] = g.astype(F32).reshape(y1 - y0, x1 - x0, Z, L)
     copies = send_halo(EX_FINE, pad2, N2, 1)
 
-    grad = tn(x3[...].reshape(-1, 3 * L), g3f[...].reshape(-1, 3 * L))
+    grad = tn(q[start:at, :], grim[...])
     for k in range(3):
-        b0, b1, b2 = [grad[k * L : k * L + C2, j * L : (j + 1) * L] for j in range(3)]
+        b0, b1, b2 = [
+            gsum[k * L : k * L + C2, j * L : (j + 1) * L] + grad[(j * 3 + k) * L : (j * 3 + k) * L + C2]
+            for j in range(3)
+        ]
         lane = lanes(b0.shape)
         r1, r2 = pltpu.roll(b1, C2, 1), pltpu.roll(b2, 2 * C2 - L, 1)
         arf32[2 * k * C2 : (2 * k + 1) * C2, :] = jnp.where(lane < C2, b0, r1)
         arf32[(2 * k + 1) * C2 : (2 * k + 2) * C2, :] = jnp.where(lane < 2 * C2 - L, r1, r2)
     arf32[6 * C2 :, :] = jnp.zeros((ROWS_F - 6 * C2, L), F32)
     f0[...] = arf32[...].astype(BF)
-    red_f = Reduce(ring, ROWS_F, (f0, f1), (fr0, fr1), fslot, fout, f_send, f_recv, sent)
+    red_f = Reduce(ring, ROWS_F, ("dp", "xy"), (f0, f1), (fr0, fr1), fslot, fout, f_send, f_recv, sent)
     red_f.scatter_start(0)
     red_m.scatter_end(1)
     red_m.last_start()
@@ -506,12 +548,12 @@
     red_f.scatter_start(1)
 
     two = c2[1 : N3 + 1, 1 : N3 + 1].reshape(-1, L).astype(BF)
-    gup[0:N3, 0:N3] = rounded(nt(two, wl[...])).reshape(N3, N3, Z, L)
+    up[...] = rounded(nt(two, wl[...])).reshape(N3, N3, Z, L)
 
     def mix(y, _):
         act = fa[pl.ds(y * 2, 2)].reshape(2, N3, 2, Z, L)
-        up = gup[pl.ds(y, 1), 0:N3].reshape(1, N3, 1, Z, L)
-        d32[pl.ds(y * 2, 2)] = (act + up).reshape(2, N2, Z, L)
+        lifted = up[pl.ds(y, 1)].reshape(1, N3, 1, Z, L)
+        d32[pl.ds(y * 2, 2)] = (act + lifted).reshape(2, N2, Z, L)
         return 0
 
     lax.fori_loop(0, N3, mix, 0)
@@ -522,8 +564,7 @@
     red_m.gather_start(1)
 
     write_cells(d32, raw, mixed_ref)
-    stores = [pltpu.make_async_copy(mixed_ref, mixed_hbm, out_sem.at[0])]
-    stores[0].start()
+    store(mixed_ref, mixed_hbm)
 
     red_f.scatter_end(1)
     red_f.last_start()
@@ -543,8 +584,7 @@
     red_f.gather_start(1)
 
     write_cells(d32, raw2, ig_ref)
-    stores.append(pltpu.make_async_copy(ig_ref, ig_hbm, out_sem.at[1]))
-    stores[1].start()
+    store(ig_ref, ig_hbm)
 
     red_m.gather_end()
     red_m.gather_start(0)
@@ -552,37 +592,66 @@
     red_e.gather_start(0)
     red_f.gather_end()
     red_f.gather_start(0)
-    for c in stores:
-        c.wait()
     red_m.gather_end()
-    red_e.gather_end()
-    red_f.gather_end()
-    for c in sent:
-        c.wait_send()
-
-
-def finish(mixed_in, ig_in, mout, eout, fout, mixed, ig, gf_ref, ge_ref, gm_ref, gl_ref, are32, arf32, sem):
-    copies = [
-        pltpu.make_async_copy(mixed_in, mixed, sem.at[0]),
-        pltpu.make_async_copy(ig_in, ig, sem.at[1]),
-    ]
-    for c in copies:
-        c.start()
     for g in range(7):
         d = [mout[(g * 3 + s) * C3 : (g * 3 + s + 1) * C3, :].astype(F32) for s in range(3)]
         for s, b in enumerate(unpack4(d)):
-            t = g * 4 + s
-            if t < 27:
-                gm_ref[t // 9, (t // 3) % 3, t % 3] = b[:, 0:C3]
-            else:
-                gl_ref[...] = b[0:C2, 0:C3]
+            mflat[(g * 4 + s) * C3 : (g * 4 + s + 1) * C3, :] = b.astype(BF)
+    store(mflat, m_hbm)
+    red_e.gather_end()
     are32[...] = eout[...].astype(F32)
     for g in range(7):
         d = [are32[(g * 3 + s) * C2 : (g * 3 + s + 1) * C2, :] for s in range(3)]
         for s, b in enumerate(unpack4(d)):
-            t = g * 4 + s
-            if t < 27:
-                ge_ref[t // 9, (t // 3) % 3, t % 3] = b[:, 0:C3]
+            eflat[(g * 4 + s) * PITCH : (g * 4 + s) * PITCH + C2, :] = b.astype(BF)
+    store(eflat, e_hbm)
+    red_f.gather_end()
+    store(fout, f_hbm)
+    for c in sent:
+        c.wait_send()
+    for done in stores:
+        done.wait()
+
+
+def finish(
+    mixed_in, ig_in, m_hbm, e_hbm, f_hbm, mixed, ig, gf_hbm, ge_hbm, gm_hbm, gl_hbm,
+    mixed_ref, ig_ref, mflat, eflat, fout, gf, ge, gm, gl, arf32, in_sem, out_sem,
+):
+    loads = [
+        pltpu.make_async_copy(src, dst, in_sem.at[i])
+        for i, (src, dst) in enumerate(
+            ((m_hbm, mflat), (e_hbm, eflat), (f_hbm, fout), (mixed_in, mixed_ref), (ig_in, ig_ref))
+        )
+    ]
+    stores = [
+        pltpu.make_async_copy(src, dst, out_sem.at[i])
+        for i, (src, dst) in enumerate(
+            ((mixed_ref, mixed), (ig_ref, ig), (gm, gm_hbm), (gl, gl_hbm), (ge, ge_hbm), (gf, gf_hbm))
+        )
+    ]
+    for load in loads:
+        load.start()
+
+    loads[0].wait()
+    for t in range(28):
+        b = mflat[t * C3 : (t + 1) * C3, :].astype(F32)
+        if t < 27:
+            gm[t // 9, (t // 3) % 3, t % 3] = b[:, 0:C3]
+        else:
+            gl[...] = b[0:C2, 0:C3]
+    stores[2].start()
+    stores[3].start()
+    for i in (3, 4):
+        loads[i].wait()
+        stores[i - 3].start()
+
+    loads[1].wait()
+    for t in range(27):
+        b = eflat[t * PITCH : t * PITCH + C2, :].astype(F32)
+        ge[t // 9, (t // 3) % 3, t % 3] = b[:, 0:C3]
+    stores[4].start()
+
+    loads[2].wait()
     arf32[...] = fout[...].astype(F32)
     for k in range(3):
         d0 = arf32[2 * k * C2 : (2 * k + 1) * C2, :]
@@ -591,17 +660,18 @@
         b1 = pltpu.roll(jnp.where(lane >= C2, d0, d1), L - C2, 1)
         b2 = pltpu.roll(d1, 2 * L - 2 * C2, 1)
         for j, b in enumerate((d0, b1, b2)):
-            gf_ref[j, k] = b[:, 0:C2]
-    for c in copies:
-        c.wait()
+            gf[j, k] = b[:, 0:C2]
+    stores[5].start()
+    for done in stores:
+        done.wait()
 
 
 def body(fine_input, fine_weight, entry_weight, middle_weight, lift_weight, upstream):
     args = (fine_input, fine_weight, entry_weight, middle_weight, lift_weight.T, upstream)
     field = jax.ShapeDtypeStruct(fine_input.shape, BF)
-    vmem = pl.BlockSpec(memory_space=pltpu.VMEM)
     whole = pl.BlockSpec(memory_space=pl.ANY)
     cells3 = (N3 + 4) * (N3 + 4) * Z
+    flat = [(28 * C3, L), (28 * PITCH, L), (ROWS_F, L)]
 
     def v(*shape):
         return pltpu.VMEM(shape, BF)
@@ -612,31 +682,33 @@
     def sems(n):
         return [pltpu.SemaphoreType.DMA((n,)), pltpu.SemaphoreType.DMA((n,))]
 
-    def sums(rows):
-        return [
-            v(rows, L), v(rows // 2, L),
-            v(1, rows // 2, L), v(15, rows // 32, L), v(4, rows // 32, L),
-            *sems(35),
-        ]
+    def sums(rows, *sizes):
+        left, sent, got = rows, [], []
+        for size in sizes:
+            sent.append(v(left, L))
+            left //= size
+            got.append(v(size - 1, left, L))
+        return [*sent, *got, v(4, left, L), *sems(3 + 2 * sum(size - 1 for size in sizes))]
 
     scratch = [
-        *[v(*arg.shape) for arg in args], v(*field.shape), v(*field.shape), *sems(6),
+        *[v(*arg.shape) for arg in args], v(*field.shape), v(*field.shape),
+        *[v(rows, L) for rows in ROWS], v(*flat[0]), v(*flat[1]), *sems(6),
         w(TILES, Z * N2, L), w(TILES, Z * N2, L), w(N2 + 2, N2 + 2, Z, L), w(N3 + 6, N3 + 6, Z, L),
         w(N3 + 2, N3 + 2, Z, L), w(N2, N2, Z, L),
         v(N2 + 2, N2 * Z, 3 * L), v(N2 + 2, N2 * Z, 3 * L), w(N2, N2, Z, L),
         v(cells3, 9 * L), w(N3 + 4, N3 + 4, Z, L), w(N3 + 2, N3 + 2, Z, L), w(N3 + 2, N3 + 2, Z, L),
-        w(N3 + 2, N3 + 2, Z, L), w(N2, N2, Z, L),
+        w(N3 + 2, N3 + 2, Z, L), w(N3, N3, Z, L), w(3 * L, 3 * L), v(8 * (N2 - 2) * Z, L), w(N2, N2, Z, L),
         v(9 * L, L), v(L, 9 * L), v(9 * L, 3 * L), v(3 * L, 9 * L), v(9 * L, 3 * L), v(3 * L, 9 * L), v(L, L),
         w(ROWS_E, L), w(ROWS_F, L),
         v(5, 8, 3 * N3 * Z, L), v(5, 8, 3 * N3 * Z, L), *sems(40),
-        *sums(ROWS_M), *sums(ROWS_E), *sums(ROWS_F),
+        *sums(ROWS_M, 2, 16), *sums(ROWS_E, 2, 16), *sums(ROWS_F, 2, 16),
     ]
-    packed = [jax.ShapeDtypeStruct((rows, L), BF) for rows in (ROWS_M, ROWS_E, ROWS_F)]
+    packed = [jax.ShapeDtypeStruct(size, BF) for size in flat]
     fields_and_sums = pl.pallas_call(
         kernel,
         out_shape=(field, field, *packed),
         in_specs=[whole] * 6,
-        out_specs=[whole] * 2 + [vmem] * 3,
+        out_specs=[whole] * 5,
         scratch_shapes=scratch,
         compiler_params=pltpu.CompilerParams(
             collective_id=0, has_side_effects=True, vmem_limit_bytes=60 * 1024 * 1024
@@ -652,10 +724,14 @@
             jax.ShapeDtypeStruct(middle_weight.shape, F32),
             jax.ShapeDtypeStruct(lift_weight.shape[::-1], F32),
         ),
-        in_specs=[whole] * 2 + [vmem] * 3,
-        out_specs=[whole] * 2 + [vmem] * 4,
-        scratch_shapes=[w(ROWS_E, L), w(ROWS_F, L), pltpu.SemaphoreType.DMA((2,))],
-        compiler_params=pltpu.CompilerParams(vmem_limit_bytes=32 * 1024 * 1024),
+        in_specs=[whole] * 5,
+        out_specs=[whole] * 6,
+        scratch_shapes=[
+            v(*field.shape), v(*field.shape), *[v(*size) for size in flat],
+            w(*fine_weight.shape), w(*entry_weight.shape), w(*middle_weight.shape), w(*lift_weight.shape[::-1]),
+            w(ROWS_F, L), *sems(6),
+        ],
+        compiler_params=pltpu.CompilerParams(vmem_limit_bytes=60 * 1024 * 1024),
     )(*fields_and_sums)
     return mixed, input_grad, fine, entry, middle, lift.T
 

time: 61.1 us -> 56.1 us (0.918)
  local copies, waits for them, and re-layouts: 4.86 us -> 0 us
    unnamed x10 -> x0, local copies, waits for them, and re-layouts: 4.86 us -> none
where the time goes in v3:
time: 56.1 us; the launch traced here: 56 us
  Pallas kernels  55.3 us (99%)
  between operations  0.64 us (1%)
    pallas_call x1, Pallas kernels, body(): pl.pallas_call(kernel, out_shape=(field, field, *packed), in_specs=[whole...  52.3 us
    pallas_call x1, Pallas kernels, body(): pl.pallas_call(finish, out_shape=(field, field, jax.ShapeDtypeStruct(fine...  2.99 us

profile of v3, /device:TPU:1, one launch (start us, length us, event | category | flops | bytes accessed | tf_op | source)
XLA Modules:
  0.0 56.0 jit_solution(12230182416297787673)
XLA Ops:
  0.6 52.3 %shard_map.109 = (bf16[1,8,16,1152]{3,2,1,0:T(8,128)(2,1)}, bf16[1,8,16,1152]{3,2,1,0:T(8,128)(2,1)}, bf16[2688,128]{1,0:T(8,128)(2,1)}, bf16[2240,128]{1,0:T(8,128)(2,1)}, bf16[512,128]{1,0:T(8,128)(2,1)}) custom-call(bf16[1,8,16,1152]{3,2,1,0:T(8,128)(2,1)} %a_hbm.1, bf16[3,3,72,72]{3,2,1,0:T(8,128)(2,1)} %wf_hbm.1, bf16[3,3,3,72,96]{4,3,2,1,0:T(8,128)(2,1)} %we_hbm.1, ...), custom_call_target="tpu_custom_call" | custom-call | tf_op jit(solution)/shard_map/pallas_call | solution.py:707
  53.0 3.0 %shard_map.110 = (bf16[1,8,16,1152]{3,2,1,0:T(8,128)(2,1)}, bf16[1,8,16,1152]{3,2,1,0:T(8,128)(2,1)}, f32[3,3,72,72]{3,2,1,0:T(8,128)}, f32[3,3,3,72,96]{4,3,2,1...) custom-call(bf16[1,8,16,1152]{3,2,1,0:T(8,128)(2,1)} %get-tuple-element.17.mixed_in, ...), custom_call_target="tpu_custom_call" | custom-call | tf_op jit(solution)/shard_map/pallas_call | solution.py:717

commit v4 on v3

--- a/solution.py
+++ b/solution.py
@@ -19,7 +19,7 @@
 GX = 8
 MERGED = N2 * C2
 TILES = MERGED // L
-DIRS = [(-1, 0), (1, 0), (-1, -1), (-1, 1), (1, -1), (1, 1), (0, -1), (0, 1)]
+DIRS = [(-1, -1), (-1, 1), (1, -1), (1, 1), (-1, 0), (1, 0), (0, -1), (0, 1)]
 
 EX_IN, EX_POOL, EX_LOW, EX_G1, EX_FINE = range(5)
 
@@ -27,6 +27,7 @@
 ROWS_E = 1536
 ROWS_F = 512
 ROWS = (ROWS_M, ROWS_E, ROWS_F)
+GROUPS = ("dp", "xy")
 PITCH = 80
 
 
@@ -70,48 +71,45 @@
         self.gy = lax.axis_index("gy")
         self.gx = lax.axis_index("gx")
 
+    def place(self):
+        return {"x": self.gy // 2, "y": self.gx // 2, "z": (self.gy % 2) * 2 + self.gx % 2}
+
     def member(self, kind):
         if kind == "dp":
             return self.dp
-        if kind == "y":
-            return self.gx // 2
-        if kind == "x":
-            return self.gy // 2
-        if kind == "xy":
-            return (self.gy // 2) * 4 + self.gx // 2
-        return (self.gy % 2) * 2 + self.gx % 2
+        place, m = self.place(), 0
+        for axis in kind:
+            m = m * 4 + place[axis]
+        return m
 
     def device(self, kind, p):
         if kind == "dp":
             return (p, self.gy, self.gx)
-        if kind == "y":
-            return (self.dp, self.gy, p * 2 + self.gx % 2)
-        if kind == "x":
-            return (self.dp, p * 2 + self.gy % 2, self.gx)
-        if kind == "xy":
-            return (self.dp, (p // 4) * 2 + self.gy % 2, (p % 4) * 2 + self.gx % 2)
-        return (self.dp, (self.gy // 2) * 2 + p // 2, (self.gx // 2) * 2 + p % 2)
+        place = self.place()
+        for axis in reversed(kind):
+            place[axis] = p % 4
+            p = p // 4
+        return (self.dp, place["x"] * 2 + place["z"] // 2, place["y"] * 2 + place["z"] % 2)
 
     def others(self, kind):
         m = self.member(kind)
         if kind == "dp":
             return [1 - m]
-        if kind in ("x", "y", "z"):
+        if len(kind) == 1:
             return [(m + r) % 4 for r in (2, 1, 3)]
         steps = [(2, 2), (2, 1), (1, 2), (2, 3), (3, 2), (1, 1), (1, 3), (3, 1), (3, 3)]
         steps += [(2, 0), (0, 2), (1, 0), (0, 1), (3, 0), (0, 3)]
         return [((m // 4 + x) % 4) * 4 + (m % 4 + y) % 4 for x, y in steps]
 
 
-SIZE = {"dp": 2, "x": 4, "y": 4, "xy": 16, "z": 4}
+SIZE = {"dp": 2, "x": 4, "y": 4, "z": 4, "xy": 16, "xz": 16, "yz": 16}
 
 
 class Reduce:
-    last = "z"
-
-    def __init__(self, ring, rows, scatter, bufs, recvs, slots, out, send, recv, sent):
+    def __init__(self, ring, rows, plan, back, bufs, recvs, slots, out, send, recv, sent):
         self.ring = ring
-        self.scatter = scatter
+        self.scatter, self.last = plan[:-1], plan[-1]
+        self.back = list(back)
         self.bufs = bufs
         self.recvs = recvs
         self.slots = slots
@@ -126,6 +124,7 @@
             n = self.rows[-1] // SIZE[kind]
             self.offs.append(self.offs[-1] + ring.member(kind) * n)
             self.rows.append(n)
+        self.held = self.offs[-1], n
 
     def _go(self, src, dst, device):
         i = self.used
@@ -177,12 +176,13 @@
             total = total + self.slots[r].astype(F32)
         self.out[pl.ds(pl.multiple_of(self.offs[-1], 16), self.rows[-1]), :] = total.astype(BF)
 
-    def gather_start(self, s):
-        kind, n = self.scatter[s], self.rows[s + 1]
-        part = self.out.at[pl.ds(pl.multiple_of(self.offs[s + 1], 16), n)]
+    def gather_start(self):
+        kind, (off, n) = self.back.pop(0), self.held
+        part = self.out.at[pl.ds(pl.multiple_of(off, 16), n)]
         self.now = []
         for p in self.ring.others(kind):
             self.now.append(self._go(part, part, self.ring.device(kind, p)))
+        self.held = off - self.ring.member(kind) * n, n * SIZE[kind]
 
     def gather_end(self):
         for c in self.now:
@@ -223,6 +223,12 @@
     ring = Ring()
     dp, gy, gx = ring.dp, ring.gy, ring.gx
 
+    barrier = pltpu.get_barrier_semaphore()
+    met = [(dp, (gy + dy + GY) % GY, (gx + dx + GX) % GX) for dy, dx in DIRS]
+    met += [ring.device(kind, p) for kind in GROUPS for p in ring.others(kind)]
+    for device in met:
+        pl.semaphore_signal(barrier, inc=1, device_id=device, device_id_type=MESH)
+
     loads = [
         pltpu.make_async_copy(src, dst, in_sem.at[i])
         for i, (src, dst) in enumerate(
@@ -234,12 +240,6 @@
     ]
     for load in loads:
         load.start()
-
-    barrier = pltpu.get_barrier_semaphore()
-    met = [(dp, (gy + dy + GY) % GY, (gx + dx + GX) % GX) for dy, dx in DIRS]
-    met += [ring.device(kind, p) for kind in ("dp", "xy") for p in ring.others(kind)]
-    for device in met:
-        pl.semaphore_signal(barrier, inc=1, device_id=device, device_id_type=MESH)
 
     sent = []
     stores = []
@@ -456,9 +456,19 @@
     take_halo(EX_LOW, ulp, N3, 1, low_copies)
     back = nn(ulp[...].reshape(-1, L).astype(BF), wl[...]).reshape(-1, Z, L)
     gp[...] = rounded(back * slope(two)).reshape(N3 + 2, N3 + 2, Z, L)
-    own = c1p[2 : N3 + 2, 2 : N3 + 2].reshape(-1, Z, L)
-    g1 = rounded(joined(nt(columns(gp, N3), wmt[...])) * slope(own))
-    gup[1 : N3 + 1, 1 : N3 + 1] = g1.reshape(N3, N3, Z, L)
+
+    def grad_one(blocks):
+        acc = joined(nt(tap_rows(gp, blocks), wmt[...]))
+        at = 0
+        for y0, y1, x0, x1 in blocks:
+            n = (y1 - y0) * (x1 - x0)
+            one = c1p[2 + y0 : 2 + y1, 2 + x0 : 2 + x1].reshape(n, Z, L)
+            g1 = rounded(acc[at : at + n] * slope(one))
+            gup[1 + y0 : 1 + y1, 1 + x0 : 1 + x1] = g1.reshape(y1 - y0, x1 - x0, Z, L)
+            at += n
+
+    inner = [(1, N3 - 1, 1, N3 - 1)]
+    grad_one(rim(N3, 1))
     copies = send_halo(EX_G1, gup, N3, 1)
 
     mid = coarse_weight_grad(
@@ -472,8 +482,9 @@
         for d, part in enumerate(pack4(blocks[4 * g : 4 * g + 4])):
             m0[(g * 3 + d) * C3 : (g * 3 + d + 1) * C3, :] = part.astype(BF)
     m0[21 * C3 :, :] = jnp.zeros((ROWS_M - 21 * C3, L), BF)
-    red_m = Reduce(ring, ROWS_M, ("dp", "xy"), (m0, m1), (mr0, mr1), mslot, mout, m_send, m_recv, sent)
+    red_m = Reduce(ring, ROWS_M, ("dp", "xy", "z"), ("xy", "dp"), (m0, m1), (mr0, mr1), mslot, mout, m_send, m_recv, sent)
     red_m.scatter_start(0)
+    grad_one(inner)
     ent = coarse_weight_grad(columns(pad3, N3, 2), gup[1 : N3 + 1, 1 : N3 + 1].reshape(-1, Z, L))
     blocks = [ent[t, :C2, i * L : (i + 1) * L] for i in range(3) for t in range(9)]
     blocks.append(jnp.zeros((C2, L), F32))
@@ -482,14 +493,16 @@
             are32[(g * 3 + d) * C2 : (g * 3 + d + 1) * C2, :] = part
     are32[21 * C2 :, :] = jnp.zeros((ROWS_E - 21 * C2, L), F32)
     e0[...] = are32[...].astype(BF)
-    red_e = Reduce(ring, ROWS_E, ("dp", "xy"), (e0, e1), (er0, er1), eslot, eout, e_send, e_recv, sent)
+    red_e = Reduce(ring, ROWS_E, ("dp", "xy", "z"), ("xy", "dp"), (e0, e1), (er0, er1), eslot, eout, e_send, e_recv, sent)
     red_e.scatter_start(0)
     red_m.scatter_end(0)
     red_m.scatter_start(1)
 
-    inner = [(1, N3 - 1, 1, N3 - 1)]
     low = rounded(joined(nt(tap_rows(gup, inner), wet[...])))
     put_rows(up, inner, 0.25 * low)
+
+    red_e.scatter_end(0)
+    red_e.scatter_start(1)
 
     def fine_back(y, _):
         act = fa[pl.ds(y * 2, 2), 2 : N2 - 2].reshape(2, N3 - 2, 2, Z, L)
@@ -502,8 +515,6 @@
         return 0
 
     lax.fori_loop(1, N3 - 1, fine_back, 0)
-    red_e.scatter_end(0)
-    red_e.scatter_start(1)
     gsum[...] = tn(x3[...].reshape(-1, 3 * L), g3f[...].reshape(-1, 3 * L))
     start = at = 4 * (N3 - 1) * Z
     for y0, y1, x0, x1 in rim(N2, 2):
@@ -526,7 +537,6 @@
         grim[rows : rows + g.shape[0], :] = g
         rows += g.shape[0]
         pad2[y0 + 1 : y1 + 1, x0 + 1 : x1 + 1] = g.astype(F32).reshape(y1 - y0, x1 - x0, Z, L)
-    copies = send_halo(EX_FINE, pad2, N2, 1)
 
     grad = tn(q[start:at, :], grim[...])
     for k in range(3):
@@ -540,12 +550,13 @@
         arf32[(2 * k + 1) * C2 : (2 * k + 2) * C2, :] = jnp.where(lane < 2 * C2 - L, r1, r2)
     arf32[6 * C2 :, :] = jnp.zeros((ROWS_F - 6 * C2, L), F32)
     f0[...] = arf32[...].astype(BF)
-    red_f = Reduce(ring, ROWS_F, ("dp", "xy"), (f0, f1), (fr0, fr1), fslot, fout, f_send, f_recv, sent)
+    red_f = Reduce(ring, ROWS_F, ("dp", "xy", "z"), ("xy", "dp"), (f0, f1), (fr0, fr1), fslot, fout, f_send, f_recv, sent)
     red_f.scatter_start(0)
+    copies = send_halo(EX_FINE, pad2, N2, 1)
+    red_f.scatter_end(0)
+    red_f.scatter_start(1)
     red_m.scatter_end(1)
     red_m.last_start()
-    red_f.scatter_end(0)
-    red_f.scatter_start(1)
 
     two = c2[1 : N3 + 1, 1 : N3 + 1].reshape(-1, L).astype(BF)
     up[...] = rounded(nt(two, wl[...])).reshape(N3, N3, Z, L)
@@ -560,16 +571,15 @@
 
     red_e.scatter_end(1)
     red_e.last_start()
+    write_cells(d32, raw, mixed_ref)
     red_m.last_end()
-    red_m.gather_start(1)
-
-    write_cells(d32, raw, mixed_ref)
+    red_m.gather_start()
     store(mixed_ref, mixed_hbm)
 
     red_f.scatter_end(1)
     red_f.last_start()
     red_e.last_end()
-    red_e.gather_start(1)
+    red_e.gather_start()
 
     take_halo(EX_FINE, pad2, N2, 1, copies)
     fine_columns()
@@ -581,17 +591,20 @@
     lax.fori_loop(0, 4, fine_backward, 0)
 
     red_f.last_end()
-    red_f.gather_start(1)
+    red_f.gather_start()
 
     write_cells(d32, raw2, ig_ref)
     store(ig_ref, ig_hbm)
+    for c in sent[:-45]:
+        c.wait_send()
+    del sent[:-45]
 
     red_m.gather_end()
-    red_m.gather_start(0)
+    red_m.gather_start()
     red_e.gather_end()
-    red_e.gather_start(0)
+    red_e.gather_start()
     red_f.gather_end()
-    red_f.gather_start(0)
+    red_f.gather_start()
     red_m.gather_end()
     for g in range(7):
         d = [mout[(g * 3 + s) * C3 : (g * 3 + s + 1) * C3, :].astype(F32) for s in range(3)]

time: 56.1 us -> 55.3 us (0.986)
  Pallas kernels: 55.3 us -> 54.5 us
    pallas_call x1, Pallas kernels: 52.3 us -> 51.5 us  [body(): pl.pallas_call(kernel, out_shape=(field, field, *packed), in_specs=[whole...]
where the time goes in v4:
time: 55.3 us; the launch traced here: 55.1 us
  Pallas kernels  54.5 us (99%)
  between operations  0.64 us (1%)
    pallas_call x1, Pallas kernels, body(): pl.pallas_call(kernel, out_shape=(field, field, *packed), in_specs=[whole...  51.5 us
    pallas_call x1, Pallas kernels, body(): pl.pallas_call(finish, out_shape=(field, field, jax.ShapeDtypeStruct(fine...  2.99 us

profile of v4, /device:TPU:1, one launch (start us, length us, event | category | flops | bytes accessed | tf_op | source)
XLA Modules:
  0.0 55.1 jit_solution(550178324213026916)
XLA Ops:
  0.6 51.5 %shard_map.109 = (bf16[1,8,16,1152]{3,2,1,0:T(8,128)(2,1)}, bf16[1,8,16,1152]{3,2,1,0:T(8,128)(2,1)}, bf16[2688,128]{1,0:T(8,128)(2,1)}, bf16[2240,128]{1,0:T(8,128)(2,1)}, bf16[512,128]{1,0:T(8,128)(2,1)}) custom-call(bf16[1,8,16,1152]{3,2,1,0:T(8,128)(2,1)} %a_hbm.1, bf16[3,3,72,72]{3,2,1,0:T(8,128)(2,1)} %wf_hbm.1, bf16[3,3,3,72,96]{4,3,2,1,0:T(8,128)(2,1)} %we_hbm.1, ...), custom_call_target="tpu_custom_call" | custom-call | tf_op jit(solution)/shard_map/pallas_call | solution.py:720
  52.2 3.0 %shard_map.110 = (bf16[1,8,16,1152]{3,2,1,0:T(8,128)(2,1)}, bf16[1,8,16,1152]{3,2,1,0:T(8,128)(2,1)}, f32[3,3,72,72]{3,2,1,0:T(8,128)}, f32[3,3,3,72,96]{4,3,2,1...) custom-call(bf16[1,8,16,1152]{3,2,1,0:T(8,128)(2,1)} %get-tuple-element.17.mixed_in, ...), custom_call_target="tpu_custom_call" | custom-call | tf_op jit(solution)/shard_map/pallas_call | solution.py:730

commit v5 on v4

--- a/solution.py
+++ b/solution.py
@@ -451,9 +451,9 @@
         (gx < GX - 1, slice(None), slice(N3 + 2, N3 + 4)),
     ):
         c1p[ys, xs] = c1p[ys, xs] * jnp.where(there, 1.0, 0.0).astype(F32)
+    take_halo(EX_LOW, ulp, N3, 1, low_copies)
     two = rounded(elu(joined(nn(columns(c1p, N3 + 2), wm[...]))))
     c2[...] = two.reshape(N3 + 2, N3 + 2, Z, L)
-    take_halo(EX_LOW, ulp, N3, 1, low_copies)
     back = nn(ulp[...].reshape(-1, L).astype(BF), wl[...]).reshape(-1, Z, L)
     gp[...] = rounded(back * slope(two)).reshape(N3 + 2, N3 + 2, Z, L)
 
@@ -572,12 +572,12 @@
     red_e.scatter_end(1)
     red_e.last_start()
     write_cells(d32, raw, mixed_ref)
+    store(mixed_ref, mixed_hbm)
+
+    red_f.scatter_end(1)
+    red_f.last_start()
     red_m.last_end()
     red_m.gather_start()
-    store(mixed_ref, mixed_hbm)
-
-    red_f.scatter_end(1)
-    red_f.last_start()
     red_e.last_end()
     red_e.gather_start()
 
@@ -630,41 +630,43 @@
     mixed_in, ig_in, m_hbm, e_hbm, f_hbm, mixed, ig, gf_hbm, ge_hbm, gm_hbm, gl_hbm,
     mixed_ref, ig_ref, mflat, eflat, fout, gf, ge, gm, gl, arf32, in_sem, out_sem,
 ):
-    loads = [
-        pltpu.make_async_copy(src, dst, in_sem.at[i])
-        for i, (src, dst) in enumerate(
-            ((m_hbm, mflat), (e_hbm, eflat), (f_hbm, fout), (mixed_in, mixed_ref), (ig_in, ig_ref))
-        )
-    ]
-    stores = [
-        pltpu.make_async_copy(src, dst, out_sem.at[i])
-        for i, (src, dst) in enumerate(
-            ((mixed_ref, mixed), (ig_ref, ig), (gm, gm_hbm), (gl, gl_hbm), (ge, ge_hbm), (gf, gf_hbm))
-        )
-    ]
+    mid, low = 9 * C3, 9 * PITCH
+    ends = (mid, 2 * mid, 28 * C3)
+    parts = [(mixed_in, mixed_ref), (ig_in, ig_ref)]
+    for i in range(3):
+        rows = pl.ds(i * mid, ends[i] - i * mid)
+        parts.append((m_hbm.at[rows], mflat.at[rows]))
+    for i in range(3):
+        parts.append((e_hbm.at[pl.ds(i * low, low)], eflat.at[pl.ds(i * low, low)]))
+    parts.append((f_hbm, fout))
+    loads = [pltpu.make_async_copy(src, dst, in_sem.at[i]) for i, (src, dst) in enumerate(parts)]
     for load in loads:
         load.start()
-
-    loads[0].wait()
-    for t in range(28):
-        b = mflat[t * C3 : (t + 1) * C3, :].astype(F32)
-        if t < 27:
-            gm[t // 9, (t // 3) % 3, t % 3] = b[:, 0:C3]
-        else:
-            gl[...] = b[0:C2, 0:C3]
-    stores[2].start()
-    stores[3].start()
-    for i in (3, 4):
+    parts = [(mixed_ref, mixed), (ig_ref, ig)]
+    parts += [(gm.at[i], gm_hbm.at[i]) for i in range(3)]
+    parts += [(ge.at[i], ge_hbm.at[i]) for i in range(3)]
+    parts += [(gf, gf_hbm), (gl, gl_hbm)]
+    stores = [pltpu.make_async_copy(src, dst, out_sem.at[i]) for i, (src, dst) in enumerate(parts)]
+
+    for i in range(2):
         loads[i].wait()
-        stores[i - 3].start()
-
-    loads[1].wait()
-    for t in range(27):
-        b = eflat[t * PITCH : t * PITCH + C2, :].astype(F32)
-        ge[t // 9, (t // 3) % 3, t % 3] = b[:, 0:C3]
-    stores[4].start()
-
-    loads[2].wait()
+        stores[i].start()
+    for i in range(3):
+        loads[2 + i].wait()
+        for t in range(9):
+            at = (i * 9 + t) * C3
+            gm[i, t // 3, t % 3] = mflat[at : at + C3, :].astype(F32)[:, 0:C3]
+        stores[2 + i].start()
+    gl[...] = mflat[27 * C3 :, :].astype(F32)[0:C2, 0:C3]
+    stores[9].start()
+    for i in range(3):
+        loads[5 + i].wait()
+        for t in range(9):
+            at = (i * 9 + t) * PITCH
+            ge[i, t // 3, t % 3] = eflat[at : at + C2, :].astype(F32)[:, 0:C3]
+        stores[5 + i].start()
+
+    loads[8].wait()
     arf32[...] = fout[...].astype(F32)
     for k in range(3):
         d0 = arf32[2 * k * C2 : (2 * k + 1) * C2, :]
@@ -674,7 +676,7 @@
         b2 = pltpu.roll(d1, 2 * L - 2 * C2, 1)
         for j, b in enumerate((d0, b1, b2)):
             gf[j, k] = b[:, 0:C2]
-    stores[5].start()
+    stores[8].start()
     for done in stores:
         done.wait()
 
@@ -742,7 +744,7 @@
         scratch_shapes=[
             v(*field.shape), v(*field.shape), *[v(*size) for size in flat],
             w(*fine_weight.shape), w(*entry_weight.shape), w(*middle_weight.shape), w(*lift_weight.shape[::-1]),
-            w(ROWS_F, L), *sems(6),
+            w(ROWS_F, L), *sems(10),
         ],
         compiler_params=pltpu.CompilerParams(vmem_limit_bytes=60 * 1024 * 1024),
     )(*fields_and_sums)

time: 55.3 us -> 55.1 us (level)
  no operation moved by 1% of the time
where the time goes in v5:
time: 55.1 us; the launch traced here: 54.9 us
  Pallas kernels  54.3 us (99%)
  between operations  0.64 us (1%)
    pallas_call x1, Pallas kernels, body(): pl.pallas_call(kernel, out_shape=(field, field, *packed), in_specs=[whole...  51.4 us
    pallas_call x1, Pallas kernels, body(): pl.pallas_call(finish, out_shape=(field, field, jax.ShapeDtypeStruct(fine...  2.84 us

profile of v5, /device:TPU:1, one launch (start us, length us, event | category | flops | bytes accessed | tf_op | source)
XLA Modules:
  0.0 54.9 jit_solution(1981263601759798855)
XLA Ops:
  0.6 51.4 %shard_map.109 = (bf16[1,8,16,1152]{3,2,1,0:T(8,128)(2,1)}, bf16[1,8,16,1152]{3,2,1,0:T(8,128)(2,1)}, bf16[2688,128]{1,0:T(8,128)(2,1)}, bf16[2240,128]{1,0:T(8,128)(2,1)}, bf16[512,128]{1,0:T(8,128)(2,1)}) custom-call(bf16[1,8,16,1152]{3,2,1,0:T(8,128)(2,1)} %a_hbm.1, bf16[3,3,72,72]{3,2,1,0:T(8,128)(2,1)} %wf_hbm.1, bf16[3,3,3,72,96]{4,3,2,1,0:T(8,128)(2,1)} %we_hbm.1, ...), custom_call_target="tpu_custom_call" | custom-call | tf_op jit(solution)/shard_map/pallas_call | solution.py:722
  52.1 2.8 %shard_map.110 = (bf16[1,8,16,1152]{3,2,1,0:T(8,128)(2,1)}, bf16[1,8,16,1152]{3,2,1,0:T(8,128)(2,1)}, f32[3,3,72,72]{3,2,1,0:T(8,128)}, f32[3,3,3,72,96]{4,3,2,1...) custom-call(bf16[1,8,16,1152]{3,2,1,0:T(8,128)(2,1)} %get-tuple-element.17.mixed_in, ...), custom_call_target="tpu_custom_call" | custom-call | tf_op jit(solution)/shard_map/pallas_call | solution.py:732

commit v6 on v5

--- a/solution.py
+++ b/solution.py
@@ -290,7 +290,7 @@
 
     def spread(src_ref):
         for t in range(TILES):
-            raw[t] = src_ref[0, :, :, t * L : (t + 1) * L].astype(F32).reshape(Z * N2, L)
+            raw[t, 0 : Z * N2] = src_ref[0, :, :, t * L : (t + 1) * L].astype(F32).reshape(Z * N2, L)
 
     def read_row(y, xs, dst, shift):
         lane = lanes((Z, L))
@@ -329,7 +329,7 @@
 
         lax.fori_loop(0, N2, row, 0)
         for t in range(TILES):
-            dst_ref[0, :, :, t * L : (t + 1) * L] = out32[t].reshape(Z, N2, L).astype(BF)
+            dst_ref[0, :, :, t * L : (t + 1) * L] = out32[t, 0 : Z * N2].reshape(Z, N2, L).astype(BF)
 
     def fine_columns():
         def row(y, _):
@@ -708,7 +708,7 @@
     scratch = [
         *[v(*arg.shape) for arg in args], v(*field.shape), v(*field.shape),
         *[v(rows, L) for rows in ROWS], v(*flat[0]), v(*flat[1]), *sems(6),
-        w(TILES, Z * N2, L), w(TILES, Z * N2, L), w(N2 + 2, N2 + 2, Z, L), w(N3 + 6, N3 + 6, Z, L),
+        w(TILES, (Z + 1) * N2, L), w(TILES, (Z + 1) * N2, L), w(N2 + 2, N2 + 2, Z, L), w(N3 + 6, N3 + 6, Z, L),
         w(N3 + 2, N3 + 2, Z, L), w(N2, N2, Z, L),
         v(N2 + 2, N2 * Z, 3 * L), v(N2 + 2, N2 * Z, 3 * L), w(N2, N2, Z, L),
         v(cells3, 9 * L), w(N3 + 4, N3 + 4, Z, L), w(N3 + 2, N3 + 2, Z, L), w(N3 + 2, N3 + 2, Z, L),

time: 55.1 us -> 55.1 us (level)
  no operation moved by 1% of the time
where the time goes in v6:
time: 55.1 us; the launch traced here: 54.9 us
  Pallas kernels  54.3 us (99%)
  between operations  0.64 us (1%)
    pallas_call x1, Pallas kernels, body(): pl.pallas_call(kernel, out_shape=(field, field, *packed), in_specs=[whole...  51.4 us
    pallas_call x1, Pallas kernels, body(): pl.pallas_call(finish, out_shape=(field, field, jax.ShapeDtypeStruct(fine...  2.84 us

profile of v6, /device:TPU:1, one launch (start us, length us, event | category | flops | bytes accessed | tf_op | source)
XLA Modules:
  0.0 54.9 jit_solution(781964426690096063)
XLA Ops:
  0.6 51.4 %shard_map.109 = (bf16[1,8,16,1152]{3,2,1,0:T(8,128)(2,1)}, bf16[1,8,16,1152]{3,2,1,0:T(8,128)(2,1)}, bf16[2688,128]{1,0:T(8,128)(2,1)}, bf16[2240,128]{1,0:T(8,128)(2,1)}, bf16[512,128]{1,0:T(8,128)(2,1)}) custom-call(bf16[1,8,16,1152]{3,2,1,0:T(8,128)(2,1)} %a_hbm.1, bf16[3,3,72,72]{3,2,1,0:T(8,128)(2,1)} %wf_hbm.1, bf16[3,3,3,72,96]{4,3,2,1,0:T(8,128)(2,1)} %we_hbm.1, ...), custom_call_target="tpu_custom_call" | custom-call | tf_op jit(solution)/shard_map/pallas_call | solution.py:722
  52.1 2.8 %shard_map.110 = (bf16[1,8,16,1152]{3,2,1,0:T(8,128)(2,1)}, bf16[1,8,16,1152]{3,2,1,0:T(8,128)(2,1)}, f32[3,3,72,72]{3,2,1,0:T(8,128)}, f32[3,3,3,72,96]{4,3,2,1...) custom-call(bf16[1,8,16,1152]{3,2,1,0:T(8,128)(2,1)} %get-tuple-element.17.mixed_in, ...), custom_call_target="tpu_custom_call" | custom-call | tf_op jit(solution)/shard_map/pallas_call | solution.py:732
